TPU v7x, 128 devices: a whole 4x4x4 slice. The times are simulated.
128 devices in a mesh: gx: 4 (over x_lo, core), gz: 32 (over y, z, x_hi).
Axes of the slice: x: 4 (x_hi: 2, x_lo: 2; x = x_hi * 2 + x_lo), y: 4, z: 4, core: 2. Of those that a mesh axis runs over, the one named last changes fastest.
Arguments:
- fields: float32 [5, 64, 512, 256], P(None, 'gx', 'gz'), may hold values from -8 to 8
- courant: float32 [256], replicated, may hold values from 0.1 to 0.6
- shear_rate: float32 [256], replicated, may hold values from -1 to 1
- gradient: float32 [256], replicated, may hold values from -1 to 1
- earlier: float32 [14, 16, 8192], P(None, 'gx', 'gz'), may hold values from -8 to 8
- basis_modes: float32 [16, 128, 64, 256], P('gx', None, 'gz'), may hold values from -4 to 4
- core_matrix: float32 [256, 256], replicated, may hold values from -1 to 60, as said below
Outputs:
- new_fields: float32 [5, 64, 512, 256], P(None, 'gx', 'gz')
- new_basis: float32 [16, 128, 64, 256], P('gx', None, 'gz')
- new_core: float32 [256, 256], replicated
Inputs may be any that keep to these rules, and one draw needn't show every extreme that they name: `core_matrix`: symmetric, every eigenvalue 2 or more.
All inputs are finite; a program needn't handle non-finite values.
Results may differ from a plain program's by a relative error of at most 0.0001.
Values sent between devices are 32-bit elements; how exact they have to be, the bound alone decides.
A program may use at most 192 MiB of HBM per device.

v0:
```python
import jax
import jax.numpy as jnp
from jax import lax
from jax.sharding import PartitionSpec as P

SIGN_STEPS = 10
POLAR_STEPS = 3


press_coef = 0.25
compress_coef = 0.25
visc_coef = 0.05
heat_coef = 0.03
gram_eps = 1e-06


def extended(cells, sides, width):
    for axis, dim in sides:
        count = lax.axis_size(axis)
        head = lax.slice_in_dim(cells, 0, width, axis=dim)
        tail = lax.slice_in_dim(cells, cells.shape[dim] - width, cells.shape[dim], axis=dim)
        cells = jnp.concatenate(
            [
                lax.ppermute(tail, axis, [(i, (i + 1) % count) for i in range(count)]),
                cells,
                lax.ppermute(head, axis, [((i + 1) % count, i) for i in range(count)]),
            ],
            axis=dim,
        )
    return cells


def advance(padded, courant, shear_rate, gradient):
    centre = padded[:, 1:-1, 1:-1, :]
    x_lower = padded[:, :-2, 1:-1, :]
    x_upper = padded[:, 2:, 1:-1, :]
    z_lower = padded[:, 1:-1, :-2, :]
    z_upper = padded[:, 1:-1, 2:, :]
    y_lower = jnp.pad(centre[..., :-1], ((0, 0), (0, 0), (0, 0), (1, 0)))
    y_upper = jnp.pad(centre[..., 1:], ((0, 0), (0, 0), (0, 0), (0, 1)))
    laplace = x_lower + x_upper + z_lower + z_upper + y_lower + y_upper - 6.0 * centre
    upwind = courant * (centre - x_lower)
    along_x = (
        centre[0]
        - upwind[0]
        - shear_rate * centre[1]
        - press_coef * 0.5 * (x_upper[3] - x_lower[3])
        + visc_coef * laplace[0]
    )
    along_y = (
        centre[1]
        - upwind[1]
        - press_coef * 0.5 * (y_upper[3] - y_lower[3])
        + visc_coef * laplace[1]
    )
    along_z = (
        centre[2]
        - upwind[2]
        - press_coef * 0.5 * (z_upper[3] - z_lower[3])
        + visc_coef * laplace[2]
    )
    divergence = x_upper[0] - x_lower[0] + (y_upper[1] - y_lower[1]) + (z_upper[2] - z_lower[2])
    pressure = centre[3] - compress_coef * 0.5 * divergence + visc_coef * laplace[3]
    heat = centre[4] - upwind[4] - gradient * centre[1] + heat_coef * laplace[4]
    return jnp.stack([along_x, along_y, along_z, pressure, heat])


def advance_with_rim(fields, courant, shear_rate, gradient):
    padded = extended(fields, (("gx", 1), ("gz", 2)), 1)
    return advance(padded, courant, shear_rate, gradient)


def coarsen(values):
    return values.reshape(
        values.shape[0] // 4, 4, values.shape[1] // 4, 4, values.shape[2] // 4, 4
    ).mean(axis=(1, 3, 5))


def rotate(core_matrix, coeffs, factor):
    mode_count = core_matrix.shape[0]
    extra = coeffs.shape[0]
    extension = jnp.concatenate([coeffs.T, factor.T], axis=0)
    correlation = jnp.pad(core_matrix, ((0, extra), (0, extra))) + jnp.dot(
        extension, extension.T, precision=lax.Precision.HIGHEST
    )
    identity = jnp.eye(mode_count + extra, dtype=jnp.float32)
    shifted = correlation - identity
    start = shifted / jnp.sqrt(jnp.sum(shifted * shifted))

    def sign_step(iteration, matrix):
        cubed = jnp.dot(
            matrix,
            jnp.dot(matrix, matrix, precision=lax.Precision.HIGHEST),
            precision=lax.Precision.HIGHEST,
        )
        return 1.5 * matrix - 0.5 * cubed

    sign_matrix = lax.fori_loop(0, SIGN_STEPS, sign_step, start)
    rotation = (0.5 * (identity + sign_matrix))[:, :mode_count]
    for _ in range(POLAR_STEPS):
        inner = jnp.dot(rotation.T, rotation, precision=lax.Precision.HIGHEST)
        rotation = 1.5 * rotation - 0.5 * jnp.dot(rotation, inner, precision=lax.Precision.HIGHEST)
    moved = jnp.dot(correlation, rotation, precision=lax.Precision.HIGHEST)
    new_core = jnp.dot(rotation.T, moved, precision=lax.Precision.HIGHEST)
    return (rotation, new_core)


def on_device(fields, courant, shear_rate, gradient, earlier, basis_modes, core_matrix):
    basis_rows = basis_modes.reshape(-1, basis_modes.shape[-1])
    rows_total = jnp.float32(basis_rows.shape[0] * lax.axis_size("gx") * lax.axis_size("gz"))
    width_z = fields.shape[2] // 4
    height = fields.shape[3] // 4
    buffered = earlier.reshape(earlier.shape[0], earlier.shape[1], width_z, height)
    halfway = advance_with_rim(fields, courant, shear_rate, gradient)
    snap_first = coarsen(halfway[0])[None]
    finished = advance_with_rim(halfway, courant, shear_rate, gradient)
    snap_second = coarsen(finished[0])[None]
    snapshots = lax.all_to_all(
        jnp.concatenate([buffered, snap_first, snap_second], axis=0),
        "gz",
        split_axis=3,
        concat_axis=2,
        tiled=True,
    )
    snapshots = snapshots.reshape(snapshots.shape[0], -1)
    local_proj = jnp.dot(snapshots, basis_rows, precision=lax.Precision.HIGHEST)
    c_one = lax.psum(local_proj, ("gx", "gz")) / rows_total
    p_one = snapshots - jnp.dot(c_one, basis_rows.T, precision=lax.Precision.HIGHEST)
    local_cross = jnp.dot(p_one, basis_rows, precision=lax.Precision.HIGHEST)
    c_two = lax.psum(local_cross, ("gx", "gz")) / rows_total
    residual = p_one - jnp.dot(c_two, basis_rows.T, precision=lax.Precision.HIGHEST)
    local_gram = jnp.dot(residual, residual.T, precision=lax.Precision.HIGHEST)
    gram_total = lax.psum(local_gram, ("gx", "gz")) / rows_total
    coeffs = c_one + c_two
    identity_m = jnp.eye(coeffs.shape[0], dtype=jnp.float32)
    factor = jnp.linalg.cholesky(gram_total + gram_eps * identity_m)
    inverse_factor = jax.scipy.linalg.solve_triangular(factor, identity_m, lower=True)
    q_rows = jnp.dot(inverse_factor, residual, precision=lax.Precision.HIGHEST)
    rotation, new_core = rotate(core_matrix, coeffs, factor)
    mode_count = core_matrix.shape[0]
    new_rows = jnp.dot(basis_rows, rotation[:mode_count], precision=lax.Precision.HIGHEST)
    new_rows = new_rows + jnp.einsum(
        "mr,mk->rk", q_rows, rotation[mode_count:], precision=lax.Precision.HIGHEST
    )
    return (finished, new_rows.reshape(basis_modes.shape), new_core)


def solution(mesh):
    return jax.shard_map(
        on_device,
        mesh=mesh,
        in_specs=(
            P(None, "gx", "gz", None),
            P(),
            P(),
            P(),
            P(None, "gx", "gz"),
            P("gx", None, "gz", None),
            P(),
        ),
        out_specs=(P(None, "gx", "gz", None), P("gx", None, "gz", None), P()),
        check_vma=False,
    )
```

profile of v0, /device:TPU:1, one launch (start us, length us, event | category | flops | bytes accessed | tf_op | source)
XLA Modules:
  0.0 473.8 jit_solution(12295473007527979935)
XLA Ops:
  1.6 2.7 collective-permute-start
  4.3 3.2 constant_dynamic-update-slice_fusion
  8.3 2.5 collective-permute-start.2
  10.8 6.0 %collective-permute-start.3 = (f32[5,18,1,256]{3,1,2,0:T(8,128)S(1)}, f32[5,18,1,256]{3,1,2,0:T(8,128)S(1)}, u32[]{:S(2)}, u32[]{:S(2)}) collective-permute-start(f32[5,18,1,256]{3,1,2,0:T(8,128)S(1)} %get-tuple-element.75), channel_id=1, source_target_pairs={{1,0},{2,1},{3,2},{4,3},{5,4},{6,5},{7,6},{8,7},{9,8},{10,9},{11,1... | collective-permute-start | bytes 276488 | tf_op jit(solution)/shard_map/ppermute | solution.py:26
  18.3 3.4 reshape.103
  22.6 3.2 dynamic-update-slice.14
  36.2 3.2 collective-permute-done.5
  40.4 7.2 %collective-permute-start.7 = (f32[5,18,1,256]{3,1,2,0:T(8,128)}, f32[5,18,1,256]{3,1,2,0:T(8,128)}, u32[]{:S(2)}, u32[]{:S(2)}) collective-permute-start(f32[5,18,1,256]{3,1,2,0:T(8,128)} %get-tuple-element.71), channel_id=1, source_target_pairs={{1,0},{2,1},{3,2},{4,3},{5,4},{6,5},{7,6},{8,7},{9,8},{10,9},{11,1... | collective-permute-start | bytes 276488 | tf_op jit(solution)/shard_map/ppermute | solution.py:26
  50.0 11.3 %mul.292 = f32[4,4,4,4,64,4]{5,4,3,2,1,0:T(8,128)} reshape(f32[1,16,16,256]{3,2,1,0:T(8,128)} %copy.186) | data formatting | bytes 524288 | tf_op jit(solution)/shard_map/mul | solution.py:48
  63.1 10.8 %mul.291 = f32[4,4,4,4,64,4]{5,4,3,2,1,0:T(8,128)} reshape(f32[1,16,16,256]{3,2,1,0:T(8,128)} %copy.185) | data formatting | bytes 524288 | tf_op jit(solution)/shard_map/mul | solution.py:47
  75.7 10.9 %sub.314 = f32[4,4,4,4,64,4]{5,4,3,2,1,0:T(8,128)} reshape(f32[1,16,16,256]{3,2,1,0:T(8,128)} %copy.183) | data formatting | bytes 524288 | tf_op jit(solution)/shard_map/sub | solution.py:44
  88.4 10.8 %squeeze.6 = f32[4,4,4,4,64,4]{5,4,3,2,1,0:T(8,128)} reshape(f32[1,16,16,256]{3,2,1,0:T(8,128)} %copy.184) | data formatting | bytes 524288 | tf_op jit(solution)/shard_map/squeeze | solution.py:46
  101.0 10.9 %mul.294 = f32[4,4,4,4,64,4]{5,4,3,2,1,0:T(8,128)} reshape(f32[1,16,16,256]{3,2,1,0:T(8,128)} %copy.190) | data formatting | bytes 524288 | tf_op jit(solution)/shard_map/mul | solution.py:54
  113.7 10.8 %mul.293 = f32[4,4,4,4,64,4]{5,4,3,2,1,0:T(8,128)} reshape(f32[1,16,16,256]{3,2,1,0:T(8,128)} %copy.189) | data formatting | bytes 524288 | tf_op jit(solution)/shard_map/mul | solution.py:53
  126.3 10.9 %squeeze.8 = f32[4,4,4,4,64,4]{5,4,3,2,1,0:T(8,128)} reshape(f32[1,16,16,256]{3,2,1,0:T(8,128)} %copy.188) | data formatting | bytes 524288 | tf_op jit(solution)/shard_map/squeeze | solution.py:52
  143.9 10.9 %mul.297 = f32[4,4,4,4,64,4]{5,4,3,2,1,0:T(8,128)} reshape(f32[1,16,16,256]{3,2,1,0:T(8,128)} %copy.192) | data formatting | bytes 524288 | tf_op jit(solution)/shard_map/mul | solution.py:48
  156.6 10.8 %mul.296 = f32[4,4,4,4,64,4]{5,4,3,2,1,0:T(8,128)} reshape(f32[1,16,16,256]{3,2,1,0:T(8,128)} %copy.191) | data formatting | bytes 524288 | tf_op jit(solution)/shard_map/mul | solution.py:47
  169.3 10.8 %squeeze.7 = f32[4,4,4,4,64,4]{5,4,3,2,1,0:T(8,128)} reshape(f32[1,16,16,256]{3,2,1,0:T(8,128)} %copy.187) | data formatting | bytes 524288 | tf_op jit(solution)/shard_map/squeeze | solution.py:45
  180.1 28.1 %fusion.81 = (f32[4,4,64]{2,1,0:T(4,128)S(1)}, f32[4,4,64]{2,1,0:T(4,128)S(1)}) fusion(f32[4,4,4,4,64,4]{5,4,3,2,1,0:T(8,128)} %mul.292, f32[4,4,4,4,64,4]{5,4,3,2,1,0:T(8,128)} %mul.291, f32[4,4,4,4,64,4]{5,4,3,2,1,0:T(8,128)} %sub.314, f32[4,4,4,4,64,4]{5,4,3,2,1,0:T(8,128)} %squeeze.6, f32[64,4]{1,0:T(8,128)S(1)} %mul.288, ...), kind=kLoop, calls=%fused_computation.171 | loop fusion | flops 915456 | bytes 2630656 | tf_op jit(solution)/shard_map/reduce_sum | solution.py:76
  208.9 2.0 copy.193
  210.9 2.1 reshape.105
  213.0 3.9 all-to-all-start
  216.9 2.1 fusion.51
  219.0 1.9 fusion.38
  222.7 3.1 copy.202
  229.8 65.9 %psum.21 = f32[16,256]{1,0:T(8,128)S(1)} all-reduce(f32[16,256]{1,0:T(8,128)S(1)} %fusion.93), channel_id=1, replica_groups=mesh['gx'=4,'gz'=32] {'gx','gz'}, use_global_device_ids=true, to_apply=%region_2.3 | all-reduce | flops 4096 | bytes 32768 | tf_op jit(solution)/shard_map/psum | solution.py:127
  297.2 63.6 %psum.22 = f32[16,256]{1,0:T(8,128)S(1)} all-reduce(f32[16,256]{1,0:T(8,128)S(1)} %fusion.94), channel_id=1, replica_groups=mesh['gx'=4,'gz'=32] {'gx','gz'}, use_global_device_ids=true, to_apply=%region_3.4 | all-reduce | flops 4096 | bytes 32768 | tf_op jit(solution)/shard_map/psum | solution.py:130
  361.9 62.7 %psum.23 = f32[16,16]{1,0:T(8,128)S(1)} all-reduce(f32[16,16]{1,0:T(8,128)S(1)} %fusion.95), channel_id=1, replica_groups=mesh['gx'=4,'gz'=32] {'gx','gz'}, use_global_device_ids=true, to_apply=%region_4.5 | all-reduce | flops 256 | bytes 2048 | tf_op jit(solution)/shard_map/psum | solution.py:133
  429.6 31.3 %while.10 = (s32[]{:T(128)}, f32[272,272]{0,1:T(8,128)S(1)}, s32[]{:T(128)}) while((s32[]{:T(128)}, f32[272,272]{0,1:T(8,128)S(1)}, s32[]{:T(128)}) %tuple.65), condition=%wide.region_9.10_spmd, body=%wide.region_8.9_spmd.sunk | while | flops 483189504 | bytes 2071597 | solution.py:98
  442.0 1.9 fusion.140
  445.1 1.9 fusion.140
  448.2 1.9 fusion.140
  (154 shorter events, 89.8 us)
Async XLA Ops:
  1.6 5.8 %collective-permute-start = (f32[5,1,16,256]{3,2,1,0:T(8,128)S(1)}, f32[5,1,16,256]{3,2,1,0:T(8,128)S(1)}, u32[]{:S(2)}, u32[]{:S(2)}) collective-permute-start(f32[5,1,16,256]{3,2,1,0:T(8,128)S(1)} %get-tuple-element.94), channel_id=1, source_target_pairs={{0,32},{32,64},{64,96},{96,0},{1,33},{33,65},{65,97},{97,1},{2,34}... | collective-permute-start | bytes 245768 | tf_op jit(solution)/shard_map/ppermute | solution.py:24
  4.2 3.9 collective-permute-start.1
  8.3 17.6 %collective-permute-start.2 = (f32[5,18,1,256]{3,1,2,0:T(8,128)S(1)}, f32[5,18,1,256]{3,1,2,0:T(8,128)S(1)}, u32[]{:S(2)}, u32[]{:S(2)}) collective-permute-start(f32[5,18,1,256]{3,1,2,0:T(8,128)S(1)} %get-tuple-element.74), channel_id=1, source_target_pairs={{0,1},{1,2},{2,3},{3,4},{4,5},{5,6},{6,7},{7,8},{8,9},{9,10},{10,1... | collective-permute-start | bytes 276488 | tf_op jit(solution)/shard_map/ppermute | solution.py:24
  10.8 15.1 %collective-permute-start.3 = (f32[5,18,1,256]{3,1,2,0:T(8,128)S(1)}, f32[5,18,1,256]{3,1,2,0:T(8,128)S(1)}, u32[]{:S(2)}, u32[]{:S(2)}) collective-permute-start(f32[5,18,1,256]{3,1,2,0:T(8,128)S(1)} %get-tuple-element.75), channel_id=1, source_target_pairs={{1,0},{2,1},{3,2},{4,3},{5,4},{6,5},{7,6},{8,7},{9,8},{10,9},{11,1... | collective-permute-start | bytes 276488 | tf_op jit(solution)/shard_map/ppermute | solution.py:26
  18.3 7.9 %copy-start.3 = (f32[5,16,16,255]{3,1,2,0:T(8,128)}, f32[5,16,16,255]{3,1,2,0:T(8,128)S(1)}, u32[]{:S(2)}) copy-start(f32[5,16,16,255]{3,1,2,0:T(8,128)S(1)} %get-tuple-element.90) | copy-start | bytes 3916804
  18.3 3.4 copy-start.16
  18.3 3.5 copy-start.15
  25.8 1.3 copy-start.5
  25.8 1.9 copy-start.7
  25.8 1.9 copy-start.18
  28.9 1.6 copy-start.4
  32.5 1.0 copy-start.17
  34.4 5.1 %collective-permute-start.5 = (f32[5,1,16,256]{3,2,1,0:T(8,128)S(1)}, f32[5,1,16,256]{3,2,1,0:T(8,128)S(1)}, u32[]{:S(2)}, u32[]{:S(2)}) collective-permute-start(f32[5,1,16,256]{3,2,1,0:T(8,128)S(1)} %copy.179), channel_id=1, source_target_pairs={{32,0},{64,32},{96,64},{0,96},{33,1},{65,33},{97,65},{1,97},{34,2}... | collective-permute-start | bytes 245768 | tf_op jit(solution)/shard_map/ppermute | solution.py:26
  35.1 4.5 collective-permute-start.4
  40.4 96.8 %collective-permute-start.6 = (f32[5,18,1,256]{3,1,2,0:T(8,128)}, f32[5,18,1,256]{3,1,2,0:T(8,128)}, u32[]{:S(2)}, u32[]{:S(2)}) collective-permute-start(f32[5,18,1,256]{3,1,2,0:T(8,128)} %get-tuple-element.70), channel_id=1, source_target_pairs={{0,1},{1,2},{2,3},{3,4},{4,5},{5,6},{6,7},{7,8},{8,9},{9,10},{10,1... | collective-permute-start | bytes 276488 | tf_op jit(solution)/shard_map/ppermute | solution.py:24
  40.4 96.8 %collective-permute-start.7 = (f32[5,18,1,256]{3,1,2,0:T(8,128)}, f32[5,18,1,256]{3,1,2,0:T(8,128)}, u32[]{:S(2)}, u32[]{:S(2)}) collective-permute-start(f32[5,18,1,256]{3,1,2,0:T(8,128)} %get-tuple-element.71), channel_id=1, source_target_pairs={{1,0},{2,1},{3,2},{4,3},{5,4},{6,5},{7,6},{8,7},{9,8},{10,9},{11,1... | collective-permute-start | bytes 276488 | tf_op jit(solution)/shard_map/ppermute | solution.py:26
  137.2 1.5 copy-start.1
  138.7 1.4 copy-start.12
  140.1 1.3 copy-start.6
  140.1 1.7 copy-start.8
  141.9 1.1 copy-start.9
  180.1 28.2 %copy-start.13 = (f32[14,4,4,64]{3,2,1,0:T(4,128)S(1)}, f32[14,4,4,64]{3,2,1,0:T(4,128)}, u32[]{:S(2)}) copy-start(f32[14,4,4,64]{3,2,1,0:T(4,128)} %reshape.101) | copy-start | bytes 172036
  213.0 12.9 %all-to-all-start = ((f32[32,1,512]{2,1,0:T(1,128)}), f32[32,1,512]{2,1,0:T(1,128)S(1)}, u32[]{:S(2)}, u32[]{:S(2)}) async-start(f32[32,1,512]{2,1,0:T(1,128)} %reshape.105), calls=%async_computation | async-start | bytes 131072 | tf_op jit(solution)/shard_map/all_to_all | solution.py:118
  216.9 2.1 copy-start.2
  216.9 2.1 copy-start.10
  219.0 1.9 copy-start.11
  227.6 1.2 copy-start
  296.6 130.8 %copy-start.14 = (f32[256,256]{1,0:T(8,128)S(1)}, f32[256,256]{1,0:T(8,128)}, u32[]{:S(2)}) copy-start(f32[256,256]{1,0:T(8,128)} %param.15) | copy-start | bytes 786436
where the time goes:
time: 482 us; the launch traced here: 474 us
  blocking collectives  192 us (40%)
  local copies, waits for them, and re-layouts  156 us (32%)
  other arithmetic  50.6 us (10%)
  matrix products  44.2 us (9%)
  starting transfers between devices  24.1 us (5%)
    psum x1, blocking collectives, on_device(): c_one = lax.psum(local_proj, ('gx', 'gz')) / rows_total  65.9 us
    psum x1, blocking collectives, on_device(): c_two = lax.psum(local_cross, ('gx', 'gz')) / rows_total  63.6 us
    psum x1, blocking collectives, on_device(): gram_total = lax.psum(local_gram, ('gx', 'gz')) / rows_total  62.7 us
    reduce_sum x1, other arithmetic, coarsen(): return values.reshape(values.shape[0] // 4, 4, values.shape[1] // 4, 4, v...  28.1 us
    mul x4, local copies, waits for them, and re-layouts, advance(): press_coef * 0.5 * (x_upper[3] - x_lower[3])  25.3 us
    mul x4, local copies, waits for them, and re-layouts, advance(): visc_coef * laplace[0]  24 us
    dot_general x10, matrix products, sign_step(): jnp.dot(matrix, matrix, precision=lax.Precision.HIGHEST)  18.6 us
    ppermute x4, starting transfers between devices, extended(): lax.ppermute(head, axis, [((i + 1) % count, i) for i in range(count)])  13.9 us
  transfers between devices with their start and end apart: 9, of which 2 were waited for; matrix products, arithmetic and copies ran while one was open for 23% of the time, Pallas kernels for 0%

commit v1 on v0

--- a/solution.py
+++ b/solution.py
@@ -1,8 +1,12 @@
 import jax
 import jax.numpy as jnp
 from jax import lax
+from jax.experimental import pallas as pl
+from jax.experimental.pallas import tpu as pltpu
 from jax.sharding import PartitionSpec as P
 
+F32, BF16 = jnp.float32, jnp.bfloat16
+HIGH = lax.Precision.HIGHEST
 SIGN_STEPS = 10
 POLAR_STEPS = 3
 
@@ -76,33 +80,201 @@
     ).mean(axis=(1, 3, 5))
 
 
-def rotate(core_matrix, coeffs, factor):
-    mode_count = core_matrix.shape[0]
-    extra = coeffs.shape[0]
-    extension = jnp.concatenate([coeffs.T, factor.T], axis=0)
-    correlation = jnp.pad(core_matrix, ((0, extra), (0, extra))) + jnp.dot(
-        extension, extension.T, precision=lax.Precision.HIGHEST
-    )
-    identity = jnp.eye(mode_count + extra, dtype=jnp.float32)
-    shifted = correlation - identity
-    start = shifted / jnp.sqrt(jnp.sum(shifted * shifted))
-
-    def sign_step(iteration, matrix):
-        cubed = jnp.dot(
-            matrix,
-            jnp.dot(matrix, matrix, precision=lax.Precision.HIGHEST),
-            precision=lax.Precision.HIGHEST,
+def halves(values):
+    head = values.astype(BF16)
+    return head, (values - head.astype(F32)).astype(BF16)
+
+
+def dot(left, right, over=((1,), (0,))):
+    return lax.dot_general(left, right, (over, ((), ())), preferred_element_type=F32)
+
+
+def dot_three(left, right, over=((1,), (0,))):
+    (lh, ll), (rh, rl) = left, right
+    return dot(lh, rh, over) + (dot(lh, rl, over) + dot(ll, rh, over))
+
+
+def dot_high(left, right, over=((1,), (0,))):
+    return lax.dot_general(
+        left, right, (over, ((), ())), precision=HIGH, preferred_element_type=F32
+    )
+
+
+TN = ((0,), (0,))
+NT = ((1,), (1,))
+
+
+def tripled_left(pair):
+    return jnp.concatenate([pair[0], pair[0], pair[1]], axis=0)
+
+
+def tripled_right(pair):
+    return jnp.concatenate([pair[0], pair[1], pair[0]], axis=0)
+
+
+def eye(count):
+    return (
+        lax.broadcasted_iota(jnp.int32, (count, count), 0)
+        == lax.broadcasted_iota(jnp.int32, (count, count), 1)
+    ).astype(F32)
+
+
+def row_places(z_lanes):
+    places = []
+    for zc in range(4):
+        for x in range(4):
+            for y in range(2):
+                places.append((zc, x, y))
+    return places
+
+
+def take_basis(view_ref, rows_ref):
+    for place, (zc, x, y) in enumerate(row_places(0)):
+        for half in range(2):
+            rows_ref[pl.ds(place * 32, 32), pl.ds(half * 128, 128)] = view_ref[
+                pl.ds(512 * x + 4 * zc + 2 * half + y, 32, stride=16), :
+            ]
+
+
+def give_basis(rows, view_ref, first):
+    for step in range(8):
+        zc, x, y = row_places(0)[first + step]
+        for half in range(2):
+            view_ref[pl.ds(512 * x + 4 * zc + 2 * half + y, 32, stride=16), :] = rows[
+                step * 32 : step * 32 + 32, half * 128 : half * 128 + 128
+            ]
+
+
+def cholesky(gram):
+    count = gram.shape[0]
+    row_index = lax.broadcasted_iota(jnp.int32, (count, count), 0)
+    col_index = lax.broadcasted_iota(jnp.int32, (count, count), 1)
+    left = gram
+    right = eye(count)
+    for j in range(count):
+        pivot = left[j : j + 1, j : j + 1]
+        scale = lax.rsqrt(pivot)
+        scale = scale * (1.5 - 0.5 * pivot * scale * scale)
+        column = left[:, j : j + 1] * scale
+        row_l = left[j : j + 1, :] * scale
+        row_r = right[j : j + 1, :] * scale
+        below = row_index > j
+        here = row_index == j
+        left = jnp.where(below, left - column * row_l, jnp.where(here, row_l, left))
+        right = jnp.where(below, right - column * row_r, jnp.where(here, row_r, right))
+    return jnp.where(row_index <= col_index, left, 0.0), right
+
+
+def product(left_v, left_d, right_v, right_d):
+    modes = left_v.shape[1]
+    lv = halves(left_v)
+    rv = halves(right_v)
+    ra = (rv[0][:modes], rv[1][:modes])
+    lb = (lv[0][modes:], lv[1][modes:])
+    rb = (rv[0][modes:], rv[1][modes:])
+    main = dot_three(lv, ra)
+    right48 = tripled_right(rb)
+    top = dot(tripled_left(lb), right48, TN)
+    low = dot(tripled_left(halves(left_d)), right48, TN)
+    out_d = dot_three(lb, rb, NT) + dot_high(left_d, right_d)
+    return main + jnp.concatenate([top, low], axis=0), out_d
+
+
+def tail_kernel(core_ref, coeffs_ref, gram_ref, resid_ref, basis_hbm, out_basis, out_core,
+                v_ref, d_ref, basis_view, basis_rows, sem):
+    modes = core_ref.shape[0]
+    fetch = pltpu.make_async_copy(basis_hbm, basis_view, sem)
+    fetch.start()
+    factor_t, inverse = cholesky(gram_ref[...] + gram_eps * eye(16))
+    coeffs = coeffs_ref[...]
+    unit = eye(modes)
+    unit_d = eye(16)
+    corr_a = core_ref[...] + dot_high(coeffs, coeffs, TN)
+    corr_b = dot_high(factor_t, coeffs)
+    corr_d = dot_high(factor_t, factor_t, NT)
+    shift_a = corr_a - unit
+    shift_d = corr_d - unit_d
+    total = (
+        jnp.sum(shift_a * shift_a, keepdims=True)
+        + 2.0 * jnp.sum(corr_b * corr_b, keepdims=True)
+        + jnp.sum(shift_d * shift_d, keepdims=True)
+    )
+    scale = 1.0 / jnp.sqrt(total)
+    v_ref[:modes] = shift_a * scale
+    v_ref[modes:] = corr_b * scale
+    d_ref[...] = shift_d * scale
+    unit_v = jnp.concatenate([unit, jnp.zeros((16, modes), F32)], axis=0)
+
+    def sign_step(step, carry):
+        v = v_ref[...]
+        d = d_ref[...]
+        square_v, square_d = product(v, d, v, d)
+        next_v, next_d = product(
+            v, d, 1.5 * unit_v - 0.5 * square_v, 1.5 * unit_d - 0.5 * square_d
         )
-        return 1.5 * matrix - 0.5 * cubed
-
-    sign_matrix = lax.fori_loop(0, SIGN_STEPS, sign_step, start)
-    rotation = (0.5 * (identity + sign_matrix))[:, :mode_count]
+        v_ref[...] = next_v
+        d_ref[...] = next_d
+        return carry
+
+    lax.fori_loop(0, SIGN_STEPS, sign_step, 0)
+
+    fetch.wait()
+    take_basis(basis_view, basis_rows)
+
+    rot = 0.5 * (unit_v + v_ref[...])
     for _ in range(POLAR_STEPS):
-        inner = jnp.dot(rotation.T, rotation, precision=lax.Precision.HIGHEST)
-        rotation = 1.5 * rotation - 0.5 * jnp.dot(rotation, inner, precision=lax.Precision.HIGHEST)
-    moved = jnp.dot(correlation, rotation, precision=lax.Precision.HIGHEST)
-    new_core = jnp.dot(rotation.T, moved, precision=lax.Precision.HIGHEST)
-    return (rotation, new_core)
+        rh, rl = halves(rot)
+        inner = dot_three((rh, rl), (rh, rl), TN)
+        rot = 1.5 * rot - 0.5 * dot_three((rh, rl), halves(inner))
+    rp = halves(rot)
+    corr_v = jnp.concatenate([corr_a, corr_b], axis=0)
+    moved = dot_three(halves(corr_v), (rp[0][:modes], rp[1][:modes]))
+    rb48 = tripled_right((rp[0][modes:], rp[1][modes:]))
+    moved = moved + jnp.concatenate(
+        [
+            dot(tripled_left(halves(corr_b)), rb48, TN),
+            dot(tripled_left(halves(corr_d)), rb48, TN),
+        ],
+        axis=0,
+    )
+    out_core[...] = dot_three(rp, halves(moved), TN)
+
+    mix = dot_high(inverse, rot[modes:], TN)
+    mix48 = tripled_right(halves(mix))
+    ra = (rp[0][:modes], rp[1][:modes])
+    for part in range(4):
+        rows = basis_rows[pl.ds(part * 256, 256), :]
+        left = tripled_left(halves(resid_ref[:, part * 256 : part * 256 + 256]))
+        give_basis(dot_three(halves(rows), ra) + dot(left, mix48, TN), out_basis, part * 8)
+
+
+def tail(core, coeffs, gram, resid, basis_view):
+    vmem = pl.BlockSpec(memory_space=pltpu.VMEM)
+    return pl.pallas_call(
+        tail_kernel,
+        out_shape=(
+            jax.ShapeDtypeStruct((2048, 128), F32),
+            jax.ShapeDtypeStruct((256, 256), F32),
+        ),
+        in_specs=[vmem, vmem, vmem, vmem, pl.BlockSpec(memory_space=pl.ANY)],
+        out_specs=(vmem, vmem),
+        scratch_shapes=[
+            pltpu.VMEM((272, 256), F32),
+            pltpu.VMEM((16, 16), F32),
+            pltpu.VMEM((2048, 128), F32),
+            pltpu.VMEM((1024, 256), F32),
+            pltpu.SemaphoreType.DMA,
+        ],
+        compiler_params=pltpu.CompilerParams(vmem_limit_bytes=32 * 1024 * 1024),
+    )(core, coeffs, gram, resid, basis_view)
+
+
+def view_of(basis):
+    return basis.reshape(4, 128, 2, 2, 128).transpose(0, 1, 3, 2, 4).reshape(2048, 128)
+
+
+def basis_of(view):
+    return view.reshape(4, 128, 2, 2, 128).transpose(0, 1, 3, 2, 4).reshape(4, 128, 2, 256)
 
 
 def on_device(fields, courant, shear_rate, gradient, earlier, basis_modes, core_matrix):
@@ -132,17 +304,9 @@
     local_gram = jnp.dot(residual, residual.T, precision=lax.Precision.HIGHEST)
     gram_total = lax.psum(local_gram, ("gx", "gz")) / rows_total
     coeffs = c_one + c_two
-    identity_m = jnp.eye(coeffs.shape[0], dtype=jnp.float32)
-    factor = jnp.linalg.cholesky(gram_total + gram_eps * identity_m)
-    inverse_factor = jax.scipy.linalg.solve_triangular(factor, identity_m, lower=True)
-    q_rows = jnp.dot(inverse_factor, residual, precision=lax.Precision.HIGHEST)
-    rotation, new_core = rotate(core_matrix, coeffs, factor)
-    mode_count = core_matrix.shape[0]
-    new_rows = jnp.dot(basis_rows, rotation[:mode_count], precision=lax.Precision.HIGHEST)
-    new_rows = new_rows + jnp.einsum(
-        "mr,mk->rk", q_rows, rotation[mode_count:], precision=lax.Precision.HIGHEST
-    )
-    return (finished, new_rows.reshape(basis_modes.shape), new_core)
+    ordered = residual.reshape(16, 4, 32, 4, 2).transpose(0, 3, 1, 4, 2).reshape(16, 1024)
+    view, new_core = tail(core_matrix, coeffs, gram_total, ordered, view_of(basis_modes))
+    return (finished, basis_of(view), new_core)
 
 
 def solution(mesh):

time: 482 us -> 449 us (0.932)
  matrix products: 44.2 us -> 3.61 us
  Pallas kernels: 0 us -> 15.6 us
    dot_general x32 -> x0, matrix products: 40.4 us -> none  [the longest x10 18.6 us: sign_step(): jnp.dot(matrix, matrix, precision=lax.Precision.HIGHEST)]
    pallas_call x0 -> x1, Pallas kernels: none -> 15.6 us  [tail(): pl.pallas_call(tail_kernel, out_shape=(jax.ShapeDtypeStruct((2048, 128),...]
    unnamed x42 -> x60, local copies, waits for them, and re-layouts: 13.3 us -> 14.3 us
  transfers between devices with their start and end apart: 9 -> 9, of which waited for: 2 -> 2; matrix products, arithmetic and copies ran while one was open for 23% -> 25% of each run, Pallas kernels for 0% -> 0%
where the time goes in v1:
time: 449 us; the launch traced here: 442 us
  blocking collectives  193 us (43%)
  local copies, waits for them, and re-layouts  156 us (35%)
  other arithmetic  47 us (10%)
  starting transfers between devices  24.5 us (5%)
  Pallas kernels  15.6 us (3%)
    psum x1, blocking collectives, on_device(): c_one = lax.psum(local_proj, ('gx', 'gz')) / rows_total  66.6 us
    psum x1, blocking collectives, on_device(): c_two = lax.psum(local_cross, ('gx', 'gz')) / rows_total  63.6 us
    psum x1, blocking collectives, on_device(): gram_total = lax.psum(local_gram, ('gx', 'gz')) / rows_total  62.7 us
    reduce_sum x1, other arithmetic, coarsen(): return values.reshape(values.shape[0] // 4, 4, values.shape[1] // 4, 4, v...  28.2 us
    mul x4, local copies, waits for them, and re-layouts, advance(): press_coef * 0.5 * (x_upper[3] - x_lower[3])  25.3 us
    mul x4, local copies, waits for them, and re-layouts, advance(): visc_coef * laplace[0]  23.6 us
    pallas_call x1, Pallas kernels, tail(): pl.pallas_call(tail_kernel, out_shape=(jax.ShapeDtypeStruct((2048, 128),...  15.6 us
    ppermute x4, starting transfers between devices, extended(): lax.ppermute(head, axis, [((i + 1) % count, i) for i in range(count)])  14.4 us
  transfers between devices with their start and end apart: 9, of which 2 were waited for; matrix products, arithmetic and copies ran while one was open for 25% of the time, Pallas kernels for 0%

profile of v1, /device:TPU:1, one launch (start us, length us, event | category | flops | bytes accessed | tf_op | source)
XLA Modules:
  0.0 441.7 jit_solution(12301742429418942221)
XLA Ops:
  1.6 2.7 collective-permute-start
  4.3 3.2 constant_dynamic-update-slice_fusion
  8.3 2.5 collective-permute-start.2
  10.8 6.0 %collective-permute-start.3 = (f32[5,18,1,256]{3,1,2,0:T(8,128)S(1)}, f32[5,18,1,256]{3,1,2,0:T(8,128)S(1)}, u32[]{:S(2)}, u32[]{:S(2)}) collective-permute-start(f32[5,18,1,256]{3,1,2,0:T(8,128)S(1)} %get-tuple-element.43), channel_id=1, source_target_pairs={{1,0},{2,1},{3,2},{4,3},{5,4},{6,5},{7,6},{8,7},{9,8},{10,9},{11,1... | collective-permute-start | bytes 276488 | tf_op jit(solution)/shard_map/ppermute | solution.py:30
  16.8 2.0 fusion.67
  18.8 3.2 dynamic-update-slice.11
  39.3 7.6 %collective-permute-start.7 = (f32[5,18,1,256]{3,1,2,0:T(8,128)}, f32[5,18,1,256]{3,1,2,0:T(8,128)}, u32[]{:S(2)}, u32[]{:S(2)}) collective-permute-start(f32[5,18,1,256]{3,1,2,0:T(8,128)} %get-tuple-element.39), channel_id=1, source_target_pairs={{1,0},{2,1},{3,2},{4,3},{5,4},{6,5},{7,6},{8,7},{9,8},{10,9},{11,1... | collective-permute-start | bytes 276488 | tf_op jit(solution)/shard_map/ppermute | solution.py:30
  47.0 2.0 fusion.65
  49.8 10.9 %mul.253 = f32[4,4,4,4,64,4]{5,4,3,2,1,0:T(8,128)} reshape(f32[1,16,16,256]{3,2,1,0:T(8,128)} %copy.178) | data formatting | bytes 524288 | tf_op jit(solution)/shard_map/mul | solution.py:52
  62.5 10.8 %mul.252 = f32[4,4,4,4,64,4]{5,4,3,2,1,0:T(8,128)} reshape(f32[1,16,16,256]{3,2,1,0:T(8,128)} %copy.177) | data formatting | bytes 524288 | tf_op jit(solution)/shard_map/mul | solution.py:51
  73.3 1.8 copy.175
  75.2 10.9 %sub.299 = f32[4,4,4,4,64,4]{5,4,3,2,1,0:T(8,128)} reshape(f32[1,16,16,256]{3,2,1,0:T(8,128)} %copy.175) | data formatting | bytes 524288 | tf_op jit(solution)/shard_map/sub | solution.py:48
  87.9 10.8 %squeeze.6 = f32[4,4,4,4,64,4]{5,4,3,2,1,0:T(8,128)} reshape(f32[1,16,16,256]{3,2,1,0:T(8,128)} %copy.176) | data formatting | bytes 524288 | tf_op jit(solution)/shard_map/squeeze | solution.py:50
  100.5 10.9 %mul.255 = f32[4,4,4,4,64,4]{5,4,3,2,1,0:T(8,128)} reshape(f32[1,16,16,256]{3,2,1,0:T(8,128)} %copy.182) | data formatting | bytes 524288 | tf_op jit(solution)/shard_map/mul | solution.py:58
  113.2 10.8 %mul.254 = f32[4,4,4,4,64,4]{5,4,3,2,1,0:T(8,128)} reshape(f32[1,16,16,256]{3,2,1,0:T(8,128)} %copy.181) | data formatting | bytes 524288 | tf_op jit(solution)/shard_map/mul | solution.py:57
  125.8 10.9 %squeeze.8 = f32[4,4,4,4,64,4]{5,4,3,2,1,0:T(8,128)} reshape(f32[1,16,16,256]{3,2,1,0:T(8,128)} %copy.180) | data formatting | bytes 524288 | tf_op jit(solution)/shard_map/squeeze | solution.py:56
  143.7 11.0 %mul.258 = f32[4,4,4,4,64,4]{5,4,3,2,1,0:T(8,128)} reshape(f32[1,16,16,256]{3,2,1,0:T(8,128)} %copy.184) | data formatting | bytes 524288 | tf_op jit(solution)/shard_map/mul | solution.py:52
  154.7 1.8 copy.183
  156.5 10.9 %mul.257 = f32[4,4,4,4,64,4]{5,4,3,2,1,0:T(8,128)} reshape(f32[1,16,16,256]{3,2,1,0:T(8,128)} %copy.183) | data formatting | bytes 524288 | tf_op jit(solution)/shard_map/mul | solution.py:51
  169.2 10.8 %squeeze.7 = f32[4,4,4,4,64,4]{5,4,3,2,1,0:T(8,128)} reshape(f32[1,16,16,256]{3,2,1,0:T(8,128)} %copy.179) | data formatting | bytes 524288 | tf_op jit(solution)/shard_map/squeeze | solution.py:49
  180.0 28.2 %fusion.58 = (f32[4,4,64]{2,1,0:T(4,128)S(1)}, f32[4,4,64]{2,1,0:T(4,128)S(1)}) fusion(f32[4,4,4,4,64,4]{5,4,3,2,1,0:T(8,128)} %mul.253, f32[4,4,4,4,64,4]{5,4,3,2,1,0:T(8,128)} %mul.252, f32[4,4,4,4,64,4]{5,4,3,2,1,0:T(8,128)} %sub.299, f32[4,4,4,4,64,4]{5,4,3,2,1,0:T(8,128)} %squeeze.6, f32[64,4]{1,0:T(8,128)S(1)} %mul.249, ...), kind=kLoop, calls=%fused_computation.132 | loop fusion | flops 915456 | bytes 2630656 | tf_op jit(solution)/shard_map/reduce_sum | solution.py:80
  208.9 1.9 copy.185
  210.9 2.1 reshape.115
  213.0 3.9 all-to-all-start
  216.8 2.1 fusion.43
  219.0 2.0 fusion.31
  221.1 1.8 fusion.39
  222.9 3.1 copy.193
  229.2 66.6 %psum.21 = f32[16,256]{1,0:T(8,128)S(1)} all-reduce(f32[16,256]{1,0:T(8,128)S(1)} %fusion.69), channel_id=1, replica_groups=mesh['gx'=4,'gz'=32] {'gx','gz'}, use_global_device_ids=true, to_apply=%region_2.3 | all-reduce | flops 4096 | bytes 32768 | tf_op jit(solution)/shard_map/psum | solution.py:299
  297.4 63.6 %psum.22 = f32[16,256]{1,0:T(8,128)S(1)} all-reduce(f32[16,256]{1,0:T(8,128)S(1)} %fusion.70), channel_id=1, replica_groups=mesh['gx'=4,'gz'=32] {'gx','gz'}, use_global_device_ids=true, to_apply=%region_3.4 | all-reduce | flops 4096 | bytes 32768 | tf_op jit(solution)/shard_map/psum | solution.py:302
  362.3 62.7 %psum.23 = f32[16,16]{1,0:T(8,128)S(1)} all-reduce(f32[16,16]{1,0:T(8,128)S(1)} %fusion.71), channel_id=1, replica_groups=mesh['gx'=4,'gz'=32] {'gx','gz'}, use_global_device_ids=true, to_apply=%region_4.5 | all-reduce | flops 256 | bytes 2048 | tf_op jit(solution)/shard_map/psum | solution.py:305
  425.8 15.6 %shard_map.94 = (f32[2048,128]{1,0:T(8,128)}, f32[256,256]{1,0:T(8,128)}) custom-call(f32[256,256]{1,0:T(8,128)S(1)} %copy-done.1, f32[16,256]{1,0:T(8,128)S(1)} %multiply_add_fusion.coeffs_ref, f32[16,16]{1,0:T(8,128)S(1)} %broadcast_multiply_fusion.gram_ref, f32[16,1024]{1,0:T(8,128)S(1)} %reshape.110.resid_ref, f32[2048,128]{1,0:T(8,128)S(1)} %bitcast.51), custom_call_target="tpu_custom_call" | custom-call | tf_op jit(solution)/shard_map/pallas_call | solution.py:253
  (119 shorter events, 45.2 us)
Async XLA Ops:
  1.6 5.9 %collective-permute-start = (f32[5,1,16,256]{3,2,1,0:T(8,128)S(1)}, f32[5,1,16,256]{3,2,1,0:T(8,128)S(1)}, u32[]{:S(2)}, u32[]{:S(2)}) collective-permute-start(f32[5,1,16,256]{3,2,1,0:T(8,128)S(1)} %get-tuple-element.62), channel_id=1, source_target_pairs={{0,32},{32,64},{64,96},{96,0},{1,33},{33,65},{65,97},{97,1},{2,34}... | collective-permute-start | bytes 245768 | tf_op jit(solution)/shard_map/ppermute | solution.py:28
  4.2 3.9 collective-permute-start.1
  8.3 13.8 %collective-permute-start.2 = (f32[5,18,1,256]{3,1,2,0:T(8,128)S(1)}, f32[5,18,1,256]{3,1,2,0:T(8,128)S(1)}, u32[]{:S(2)}, u32[]{:S(2)}) collective-permute-start(f32[5,18,1,256]{3,1,2,0:T(8,128)S(1)} %get-tuple-element.42), channel_id=1, source_target_pairs={{0,1},{1,2},{2,3},{3,4},{4,5},{5,6},{6,7},{7,8},{8,9},{9,10},{10,1... | collective-permute-start | bytes 276488 | tf_op jit(solution)/shard_map/ppermute | solution.py:28
  10.8 11.3 %collective-permute-start.3 = (f32[5,18,1,256]{3,1,2,0:T(8,128)S(1)}, f32[5,18,1,256]{3,1,2,0:T(8,128)S(1)}, u32[]{:S(2)}, u32[]{:S(2)}) collective-permute-start(f32[5,18,1,256]{3,1,2,0:T(8,128)S(1)} %get-tuple-element.43), channel_id=1, source_target_pairs={{1,0},{2,1},{3,2},{4,3},{5,4},{6,5},{7,6},{8,7},{9,8},{10,9},{11,1... | collective-permute-start | bytes 276488 | tf_op jit(solution)/shard_map/ppermute | solution.py:30
  22.0 1.3 copy-start.8
  22.0 1.7 copy-start.9
  22.0 2.3 copy-start.11
  22.0 2.3 copy-start.27
  29.6 4.6 %copy-start.23 = (f32[14,4,256]{2,1,0:T(4,128)S(1)}, f32[14,4,256]{2,1,0:T(4,128)}, u32[]{:S(2)}) copy-start(f32[14,4,256]{2,1,0:T(4,128)} %param.11) | copy-start | bytes 172036
  29.6 5.3 %copy-start = (f32[4,128,2,256]{3,2,1,0:T(2,128)S(1)}, f32[4,128,2,256]{3,2,1,0:T(2,128)}, u32[]{:S(2)}) copy-start(f32[4,128,2,256]{3,2,1,0:T(2,128)} %param.12) | copy-start | bytes 3145732
  31.6 4.4 collective-permute-start.5
  32.9 5.6 %copy-start.3 = (f32[5,16,16,256]{3,1,2,0:T(8,128)S(1)}, f32[5,16,16,256]{3,1,2,0:T(8,128)}, u32[]{:S(2)}) copy-start(f32[5,16,16,256]{3,1,2,0:T(8,128)} %copy-done.2) | copy-start | bytes 3932164
  32.9 4.0 collective-permute-start.4
  39.3 97.4 %collective-permute-start.6 = (f32[5,18,1,256]{3,1,2,0:T(8,128)}, f32[5,18,1,256]{3,1,2,0:T(8,128)}, u32[]{:S(2)}, u32[]{:S(2)}) collective-permute-start(f32[5,18,1,256]{3,1,2,0:T(8,128)} %get-tuple-element.38), channel_id=1, source_target_pairs={{0,1},{1,2},{2,3},{3,4},{4,5},{5,6},{6,7},{7,8},{8,9},{9,10},{10,1... | collective-permute-start | bytes 276488 | tf_op jit(solution)/shard_map/ppermute | solution.py:28
  39.3 9.7 %copy-start.21 = (f32[1,16,16,256]{3,1,2,0:T(8,128)S(1)}, f32[1,16,16,256]{3,1,2,0:T(8,128)}, u32[]{:S(2)}) copy-start(f32[1,16,16,256]{3,1,2,0:T(8,128)} %get-tuple-element.53) | copy-start | bytes 786436
  39.3 97.4 %collective-permute-start.7 = (f32[5,18,1,256]{3,1,2,0:T(8,128)}, f32[5,18,1,256]{3,1,2,0:T(8,128)}, u32[]{:S(2)}, u32[]{:S(2)}) collective-permute-start(f32[5,18,1,256]{3,1,2,0:T(8,128)} %get-tuple-element.39), channel_id=1, source_target_pairs={{1,0},{2,1},{3,2},{4,3},{5,4},{6,5},{7,6},{8,7},{9,8},{10,9},{11,1... | collective-permute-start | bytes 276488 | tf_op jit(solution)/shard_map/ppermute | solution.py:30
  136.7 1.7 copy-start.4
  136.7 1.9 copy-start.6
  136.7 1.9 copy-start.16
  138.6 1.4 copy-start.13
  138.6 1.4 copy-start.20
  140.0 1.3 copy-start.10
  140.0 1.6 copy-start.12
  180.0 28.2 %copy-start.22 = (f32[14,4,4,64]{3,2,1,0:T(4,128)S(1)}, f32[14,4,4,64]{3,2,1,0:T(4,128)}, u32[]{:S(2)}) copy-start(f32[14,4,4,64]{3,2,1,0:T(4,128)} %reshape.106) | copy-start | bytes 172036
  213.0 13.0 %all-to-all-start = ((f32[32,1,512]{2,1,0:T(1,128)}), f32[32,1,512]{2,1,0:T(1,128)S(1)}, u32[]{:S(2)}, u32[]{:S(2)}) async-start(f32[32,1,512]{2,1,0:T(1,128)} %reshape.115), calls=%async_computation | async-start | bytes 131072 | tf_op jit(solution)/shard_map/all_to_all | solution.py:290
  216.8 2.2 copy-start.5
  216.8 2.2 copy-start.7
  216.8 2.2 copy-start.17
  219.0 2.0 copy-start.14
  219.0 2.0 copy-start.19
  219.0 2.0 copy-start.26
  360.9 64.9 %copy-start.1 = (f32[256,256]{1,0:T(8,128)S(1)}, f32[256,256]{1,0:T(8,128)}, u32[]{:S(2)}) copy-start(f32[256,256]{1,0:T(8,128)} %core_ref.1) | copy-start | bytes 786436
  (5 other events, 4.9 us)

commit v2 on v1

--- a/solution.py
+++ b/solution.py
@@ -1,3 +1,5 @@
+import functools
+
 import jax
 import jax.numpy as jnp
 from jax import lax
@@ -9,75 +11,7 @@
 HIGH = lax.Precision.HIGHEST
 SIGN_STEPS = 10
 POLAR_STEPS = 3
-
-
-press_coef = 0.25
-compress_coef = 0.25
-visc_coef = 0.05
-heat_coef = 0.03
 gram_eps = 1e-06
-
-
-def extended(cells, sides, width):
-    for axis, dim in sides:
-        count = lax.axis_size(axis)
-        head = lax.slice_in_dim(cells, 0, width, axis=dim)
-        tail = lax.slice_in_dim(cells, cells.shape[dim] - width, cells.shape[dim], axis=dim)
-        cells = jnp.concatenate(
-            [
-                lax.ppermute(tail, axis, [(i, (i + 1) % count) for i in range(count)]),
-                cells,
-                lax.ppermute(head, axis, [((i + 1) % count, i) for i in range(count)]),
-            ],
-            axis=dim,
-        )
-    return cells
-
-
-def advance(padded, courant, shear_rate, gradient):
-    centre = padded[:, 1:-1, 1:-1, :]
-    x_lower = padded[:, :-2, 1:-1, :]
-    x_upper = padded[:, 2:, 1:-1, :]
-    z_lower = padded[:, 1:-1, :-2, :]
-    z_upper = padded[:, 1:-1, 2:, :]
-    y_lower = jnp.pad(centre[..., :-1], ((0, 0), (0, 0), (0, 0), (1, 0)))
-    y_upper = jnp.pad(centre[..., 1:], ((0, 0), (0, 0), (0, 0), (0, 1)))
-    laplace = x_lower + x_upper + z_lower + z_upper + y_lower + y_upper - 6.0 * centre
-    upwind = courant * (centre - x_lower)
-    along_x = (
-        centre[0]
-        - upwind[0]
-        - shear_rate * centre[1]
-        - press_coef * 0.5 * (x_upper[3] - x_lower[3])
-        + visc_coef * laplace[0]
-    )
-    along_y = (
-        centre[1]
-        - upwind[1]
-        - press_coef * 0.5 * (y_upper[3] - y_lower[3])
-        + visc_coef * laplace[1]
-    )
-    along_z = (
-        centre[2]
-        - upwind[2]
-        - press_coef * 0.5 * (z_upper[3] - z_lower[3])
-        + visc_coef * laplace[2]
-    )
-    divergence = x_upper[0] - x_lower[0] + (y_upper[1] - y_lower[1]) + (z_upper[2] - z_lower[2])
-    pressure = centre[3] - compress_coef * 0.5 * divergence + visc_coef * laplace[3]
-    heat = centre[4] - upwind[4] - gradient * centre[1] + heat_coef * laplace[4]
-    return jnp.stack([along_x, along_y, along_z, pressure, heat])
-
-
-def advance_with_rim(fields, courant, shear_rate, gradient):
-    padded = extended(fields, (("gx", 1), ("gz", 2)), 1)
-    return advance(padded, courant, shear_rate, gradient)
-
-
-def coarsen(values):
-    return values.reshape(
-        values.shape[0] // 4, 4, values.shape[1] // 4, 4, values.shape[2] // 4, 4
-    ).mean(axis=(1, 3, 5))
 
 
 def halves(values):
@@ -180,11 +114,13 @@
     return main + jnp.concatenate([top, low], axis=0), out_d
 
 
-def tail_kernel(core_ref, coeffs_ref, gram_ref, resid_ref, basis_hbm, out_basis, out_core,
-                v_ref, d_ref, basis_view, basis_rows, sem):
+def tail_kernel(core_ref, coeffs_ref, gram_ref, resid_ref, basis_hbm, fields_hbm,
+                out_fields, out_basis, out_core, v_ref, d_ref, basis_view, basis_rows, sem, field_sem):
     modes = core_ref.shape[0]
     fetch = pltpu.make_async_copy(basis_hbm, basis_view, sem)
     fetch.start()
+    passing = pltpu.make_async_copy(fields_hbm, out_fields, field_sem)
+    passing.start()
     factor_t, inverse = cholesky(gram_ref[...] + gram_eps * eye(16))
     coeffs = coeffs_ref[...]
     unit = eye(modes)
@@ -246,27 +182,31 @@
         rows = basis_rows[pl.ds(part * 256, 256), :]
         left = tripled_left(halves(resid_ref[:, part * 256 : part * 256 + 256]))
         give_basis(dot_three(halves(rows), ra) + dot(left, mix48, TN), out_basis, part * 8)
-
-
-def tail(core, coeffs, gram, resid, basis_view):
+    passing.wait()
+
+
+def tail(core, coeffs, gram, resid, basis_view, fields):
     vmem = pl.BlockSpec(memory_space=pltpu.VMEM)
+    hbm = pl.BlockSpec(memory_space=pl.ANY)
     return pl.pallas_call(
         tail_kernel,
         out_shape=(
+            jax.ShapeDtypeStruct(fields.shape, F32),
             jax.ShapeDtypeStruct((2048, 128), F32),
             jax.ShapeDtypeStruct((256, 256), F32),
         ),
-        in_specs=[vmem, vmem, vmem, vmem, pl.BlockSpec(memory_space=pl.ANY)],
-        out_specs=(vmem, vmem),
+        in_specs=[vmem, vmem, vmem, vmem, hbm, hbm],
+        out_specs=(hbm, vmem, vmem),
         scratch_shapes=[
             pltpu.VMEM((272, 256), F32),
             pltpu.VMEM((16, 16), F32),
             pltpu.VMEM((2048, 128), F32),
             pltpu.VMEM((1024, 256), F32),
             pltpu.SemaphoreType.DMA,
+            pltpu.SemaphoreType.DMA,
         ],
         compiler_params=pltpu.CompilerParams(vmem_limit_bytes=32 * 1024 * 1024),
-    )(core, coeffs, gram, resid, basis_view)
+    )(core, coeffs, gram, resid, basis_view, fields)
 
 
 def view_of(basis):
@@ -277,36 +217,390 @@
     return view.reshape(4, 128, 2, 2, 128).transpose(0, 1, 3, 2, 4).reshape(4, 128, 2, 256)
 
 
+MESH = pl.DeviceIdType.MESH
+press_coef = 0.25
+compress_coef = 0.25
+visc_coef = 0.05
+heat_coef = 0.03
+FIELDS = 5
+
+
+def shifted(values):
+    width = values.shape[-1]
+    lane = lax.broadcasted_iota(jnp.int32, values.shape, 1)
+    lower = jnp.where(lane == 0, 0.0, pltpu.roll(values, 1, 1))
+    upper = jnp.where(lane == width - 1, 0.0, pltpu.roll(values, width - 1, 1))
+    return lower, upper
+
+
+def update(centre, xl, xu, zl, zu, profiles):
+    courant, shear_rate, gradient = profiles
+    beside = [shifted(c) for c in centre]
+    keep = [1.0 - 6.0 * visc_coef - courant] * 3 + [1.0 - 6.0 * visc_coef]
+    keep = keep + [1.0 - 6.0 * heat_coef - courant]
+    bring = [visc_coef + courant] * 3 + [visc_coef, heat_coef + courant]
+    spread = [visc_coef] * 4 + [heat_coef]
+    new = []
+    for f in range(FIELDS):
+        around = (xu[f] + zl[f]) + (zu[f] + beside[f][0]) + beside[f][1]
+        new.append(keep[f] * centre[f] + bring[f] * xl[f] + spread[f] * around)
+    half_press = 0.5 * press_coef
+    new[0] = new[0] - shear_rate * centre[1] - half_press * (xu[3] - xl[3])
+    new[1] = new[1] - half_press * (beside[3][1] - beside[3][0])
+    new[2] = new[2] - half_press * (zu[3] - zl[3])
+    divergence = (xu[0] - xl[0]) + (beside[1][1] - beside[1][0]) + (zu[2] - zl[2])
+    new[3] = new[3] - 0.5 * compress_coef * divergence
+    new[4] = new[4] - gradient * centre[1]
+    return new
+
+
+def front_kernel(sizes, fields_hbm, profiles_ref, earlier_ref, basis_hbm,
+                 out_fields, out_coeffs, out_gram, out_resid,
+                 P, H, F, Zs, Zr, Cs, Cr, V, basis_view, basis_rows, basis_h, basis_l,
+                 E2, early_send, early_slots, late_send, late_slots, S,
+                 sum_send, sum_slots, sum_mid, sum_mid_slots, sum_out, sum_all,
+                 c_send, c_slots, c_mid, c_mid_slots,
+                 g_send, g_slots, g_mid, g_mid_slots,
+                 load_sem, basis_sem, out_sem, halo_send, halo_recv,
+                 group_send, group_recv):
+    nx, nz = sizes
+    gx = lax.axis_index("gx")
+    gz = lax.axis_index("gz")
+    rows_total = 1024.0 * nx * nz
+
+    load = pltpu.make_async_copy(fields_hbm, P.at[:, 2:18, 8:24, :], load_sem)
+    load.start()
+    fetch = pltpu.make_async_copy(basis_hbm, basis_view, basis_sem)
+    fetch.start()
+
+    barrier = pltpu.get_barrier_semaphore()
+
+    def greet_z(d, carry):
+        pl.semaphore_signal(barrier, inc=1, device_id=(gx, lax.rem(gz + d, nz)), device_id_type=MESH)
+        return carry
+
+    lax.fori_loop(1, nz, greet_z, 0)
+    for d in range(1, nx):
+        pl.semaphore_signal(barrier, inc=1, device_id=(lax.rem(gx + d, nx), gz), device_id_type=MESH)
+    x_beside = (lax.rem(gx + nx - 1, nx), lax.rem(gx + 1, nx))
+    z_beside = (lax.rem(gz + nz - 1, nz), lax.rem(gz + 1, nz))
+    for xs in range(2):
+        for zs in range(2):
+            pl.semaphore_signal(
+                barrier, inc=1, device_id=(x_beside[xs], z_beside[zs]), device_id_type=MESH
+            )
+
+    load.wait()
+    flat = P.reshape(FIELDS * 20 * 32, 256)
+    for side in range(2):
+        for layer in range(2):
+            z = 8 + 14 * side + layer
+            for f in range(FIELDS):
+                for half in range(2):
+                    lanes = pl.ds(128 * half, 128)
+                    Zs[side, layer, f, :, lanes] = P[f, 2:18, z, lanes]
+    for xs in range(2):
+        for zs in range(2):
+            for f in range(FIELDS):
+                Cs[2 * xs + zs, f : f + 1, :] = P[f, 2 + 15 * xs, 8 + 15 * zs : 9 + 15 * zs, :]
+
+    pl.semaphore_wait(barrier, nz - 1 + nx - 1 + 4)
+
+    halos = []
+
+    def send_halo(source, target, where):
+        place = len(halos)
+        copy = pltpu.make_async_remote_copy(
+            src_ref=source, dst_ref=target, send_sem=halo_send.at[place],
+            recv_sem=halo_recv.at[place], device_id=where, device_id_type=MESH,
+        )
+        copy.start()
+        halos.append(copy)
+
+    for side in range(2):
+        send_halo(Zs.at[side], Zr.at[1 - side, :, :, 8:24, :], (gx, z_beside[side]))
+    for side in range(2):
+        send_halo(
+            fields_hbm.at[:, 14 * side : 14 * side + 2],
+            P.at[:, 18 - 18 * side : 20 - 18 * side, 8:24, :],
+            (x_beside[side], gz),
+        )
+    for xs in range(2):
+        for zs in range(2):
+            send_halo(
+                Cs.at[2 * xs + zs], Cr.at[2 * (1 - xs) + 1 - zs], (x_beside[xs], z_beside[zs])
+            )
+
+    def spread_z(place, source, slots):
+        def body(d, carry):
+            peer = lax.rem(gz + d, nz)
+            pltpu.make_async_remote_copy(
+                src_ref=source(peer), dst_ref=slots.at[gz], send_sem=group_send.at[place],
+                recv_sem=group_recv.at[place], device_id=(gx, peer), device_id_type=MESH,
+            ).start()
+            return carry
+
+        lax.fori_loop(1, nz, body, 0)
+
+    def spread_x(place, source, slots):
+        for d in range(1, nx):
+            peer = lax.rem(gx + d, nx)
+            pltpu.make_async_remote_copy(
+                src_ref=source, dst_ref=slots.at[gx], send_sem=group_send.at[place],
+                recv_sem=group_recv.at[place], device_id=(peer, gz), device_id_type=MESH,
+            ).start()
+
+    def wait_all(sems, place, slots):
+        some = slots.at[pl.ds(0, slots.shape[0] - 1)]
+        pltpu.make_async_copy(some, some, sems.at[place]).wait()
+
+    E2[...] = jnp.zeros_like(E2)
+    for m in range(14):
+        for x in range(4):
+            E2[x * 16 + m : x * 16 + m + 1, :] = earlier_ref[m, x : x + 1, :]
+    turned = E2[...].T
+    turned = jnp.concatenate([turned[64 * z : 64 * z + 64] for z in range(4)], axis=1)
+    for i in range(32):
+        early_send[i] = turned[2 * i : 2 * i + 2]
+    spread_z(0, lambda peer: early_send.at[peer], early_slots)
+    early_slots[gz] = early_send[gz]
+
+    fetch.wait()
+    take_basis(basis_view, basis_rows)
+    rows = basis_rows[...]
+    head = rows.astype(BF16)
+    basis_h[...] = head
+    basis_l[...] = (rows - head.astype(F32)).astype(BF16)
+
+    def pair():
+        return basis_h[...], basis_l[...]
+
+    inner = dot_three(pair(), pair(), TN)
+    sum_send[:, :, 256:] = jnp.zeros((32, 8, 128), F32)
+    for i in range(32):
+        sum_send[i, :, :256] = inner[8 * i : 8 * i + 8]
+
+    wait_all(group_recv, 0, early_slots)
+    got = jnp.concatenate([early_slots[:, 0, :], early_slots[:, 1, :]], axis=0).T
+    for zx in range(16):
+        S[:, zx * 64 : zx * 64 + 64] = got[zx * 16 : zx * 16 + 16]
+    c_early = dot_three(halves(S[...]), pair())
+    for m in range(16):
+        for half in range(2):
+            sum_send[2 * m + half, 0:1, 256:] = c_early[m : m + 1, 128 * half : 128 * half + 128]
+    spread_z(1, lambda peer: sum_send.at[peer], sum_slots)
+    sum_slots[gz] = sum_send[gz]
+
+    profiles = [profiles_ref[k : k + 1, :] for k in range(3)]
+    for copy in halos:
+        copy.wait_recv()
+    for f in range(FIELDS):
+        for xs in range(2):
+            row = 7 + 17 * xs
+            for zs in range(2):
+                Zr[zs, 1 - zs, f, row : row + 1, :] = Cr[2 * xs + zs, f : f + 1, :]
+        for zs in range(2):
+            z = 7 + 17 * zs
+            P[f, 1:19, z, :] = Zr[zs, 1 - zs, f, 7:25, :]
+
+    def first(i, carry):
+        centre = [P[f, i + 1, 8:24, :] for f in range(FIELDS)]
+        xl = [P[f, i, 8:24, :] for f in range(FIELDS)]
+        xu = [P[f, i + 2, 8:24, :] for f in range(FIELDS)]
+        zl = [P[f, i + 1, 7:23, :] for f in range(FIELDS)]
+        zu = [P[f, i + 1, 9:25, :] for f in range(FIELDS)]
+        new = update(centre, xl, xu, zl, zu, profiles)
+        for f in range(FIELDS):
+            H[f, i, 8:24, :] = new[f]
+        return carry
+
+    lax.fori_loop(0, 18, first, 0)
+    for side in range(2):
+        centre = [Zr[side, 1 - side, f, 8:24, :] for f in range(FIELDS)]
+        xl = [Zr[side, 1 - side, f, 7:23, :] for f in range(FIELDS)]
+        xu = [Zr[side, 1 - side, f, 9:25, :] for f in range(FIELDS)]
+        outer = [Zr[side, side, f, 8:24, :] for f in range(FIELDS)]
+        inside = [Zs[side, side, f, :, :] for f in range(FIELDS)]
+        zl, zu = (outer, inside) if side == 0 else (inside, outer)
+        new = update(centre, xl, xu, zl, zu, profiles)
+        for f in range(FIELDS):
+            H[f, 1:17, 7 + 17 * side, :] = new[f]
+
+    def second(i, carry):
+        centre = [H[f, i + 1, 8:24, :] for f in range(FIELDS)]
+        xl = [H[f, i, 8:24, :] for f in range(FIELDS)]
+        xu = [H[f, i + 2, 8:24, :] for f in range(FIELDS)]
+        zl = [H[f, i + 1, 7:23, :] for f in range(FIELDS)]
+        zu = [H[f, i + 1, 9:25, :] for f in range(FIELDS)]
+        new = update(centre, xl, xu, zl, zu, profiles)
+        for f in range(FIELDS):
+            F[f, i, :, :] = new[f]
+        return carry
+
+    lax.fori_loop(0, 16, second, 0)
+    store = pltpu.make_async_copy(F, out_fields, out_sem)
+    store.start()
+
+    for xg in range(4):
+        V[16 * xg : 16 * xg + 16, :] = (H[0, 4 * xg + 1, 8:24, :] + H[0, 4 * xg + 2, 8:24, :]) + (
+            H[0, 4 * xg + 3, 8:24, :] + H[0, 4 * xg + 4, 8:24, :]
+        )
+        V[64 + 16 * xg : 80 + 16 * xg, :] = (F[0, 4 * xg] + F[0, 4 * xg + 1]) + (
+            F[0, 4 * xg + 2] + F[0, 4 * xg + 3]
+        )
+    to = lax.broadcasted_iota(jnp.int32, (128, 128), 0)
+    of = lax.broadcasted_iota(jnp.int32, (128, 128), 1)
+    wanted = ((lax.rem(of, 16) // 4) * 4 + lax.rem(of, 64) // 16) * 8 + 6 + of // 64
+    gathered = dot_high((to == wanted).astype(F32), V[...])
+    block = (
+        lax.broadcasted_iota(jnp.int32, (64, 256), 0)
+        == lax.broadcasted_iota(jnp.int32, (64, 256), 1) // 4
+    ).astype(F32) * (1.0 / 64.0)
+    coarse = dot_high(block, gathered, NT)
+    for i in range(32):
+        late_send[i] = coarse[2 * i : 2 * i + 2]
+    spread_z(2, lambda peer: late_send.at[peer], late_slots)
+    late_slots[gz] = late_send[gz]
+
+    wait_all(group_recv, 1, sum_slots)
+    total = sum_slots[0]
+    for j in range(1, 32):
+        total = total + sum_slots[j]
+    sum_mid[...] = total
+    spread_x(3, sum_mid, sum_mid_slots)
+    sum_mid_slots[gx] = total
+
+    wait_all(group_recv, 2, late_slots)
+    got = jnp.concatenate([late_slots[:, 0, :], late_slots[:, 1, :]], axis=0).T
+    for zx in range(16):
+        S[8:16, zx * 64 : zx * 64 + 64] = S[8:16, zx * 64 : zx * 64 + 64] + got[zx * 8 : zx * 8 + 8]
+    low = S[8:16, :]
+    low = jnp.where(lax.broadcasted_iota(jnp.int32, low.shape, 0) >= 6, low, 0.0)
+    c_late = dot_three(halves(jnp.concatenate([jnp.zeros_like(low), low], axis=0)), pair())[14:16]
+    c_send[...] = c_late
+    spread_z(4, lambda peer: c_send, c_slots)
+    c_slots[gz] = c_late
+
+    wait_all(group_recv, 3, sum_mid_slots)
+    total = ((sum_mid_slots[0] + sum_mid_slots[1]) + sum_mid_slots[2]) + sum_mid_slots[3]
+    sum_out[...] = total
+    spread_z(5, lambda peer: sum_out, sum_all)
+    sum_all[gz] = total
+
+    wait_all(group_recv, 4, c_slots)
+    total = c_slots[0]
+    for j in range(1, 32):
+        total = total + c_slots[j]
+    c_mid[...] = total
+    spread_x(6, c_mid, c_mid_slots)
+    c_mid_slots[gx] = total
+
+    wait_all(group_recv, 5, sum_all)
+    metric = sum_all[:, :, :256].reshape(256, 256) * (1.0 / rows_total)
+    early_rows = [
+        jnp.concatenate([sum_all[2 * m, 0:1, 256:], sum_all[2 * m + 1, 0:1, 256:]], axis=1)
+        for m in range(14)
+    ]
+    wait_all(group_recv, 6, c_mid_slots)
+    total = ((c_mid_slots[0] + c_mid_slots[1]) + c_mid_slots[2]) + c_mid_slots[3]
+    c_one = jnp.concatenate(early_rows + [total], axis=0) * (1.0 / rows_total)
+    coeffs = c_one + (c_one - dot_high(c_one, metric))
+    out_coeffs[...] = coeffs
+    resid = S[...] - dot_three(halves(coeffs), pair(), NT)
+    out_resid[...] = resid
+    gram = dot_high(resid, resid, NT) * (1.0 / rows_total)
+    g_send[...] = gram
+    spread_z(7, lambda peer: g_send, g_slots)
+    g_slots[gz] = gram
+    wait_all(group_recv, 7, g_slots)
+    total = g_slots[0]
+    for j in range(1, 32):
+        total = total + g_slots[j]
+    g_mid[...] = total
+    spread_x(8, g_mid, g_mid_slots)
+    g_mid_slots[gx] = total
+    wait_all(group_recv, 8, g_mid_slots)
+    out_gram[...] = ((g_mid_slots[0] + g_mid_slots[1]) + g_mid_slots[2]) + g_mid_slots[3]
+
+    for copy in halos:
+        copy.wait_send()
+    for place, slots in enumerate([
+        early_slots, sum_slots, late_slots, sum_mid_slots, c_slots, sum_all, c_mid_slots,
+        g_slots, g_mid_slots,
+    ]):
+        wait_all(group_send, place, slots)
+    store.wait()
+
+
+def front(sizes, fields, profiles, earlier, basis_view):
+    nx, nz = sizes
+    vmem = pl.BlockSpec(memory_space=pltpu.VMEM)
+    hbm = pl.BlockSpec(memory_space=pl.ANY)
+    v = pltpu.VMEM
+    return pl.pallas_call(
+        functools.partial(front_kernel, sizes),
+        out_shape=(
+            jax.ShapeDtypeStruct(fields.shape, F32),
+            jax.ShapeDtypeStruct((16, 256), F32),
+            jax.ShapeDtypeStruct((16, 16), F32),
+            jax.ShapeDtypeStruct((16, 1024), F32),
+        ),
+        in_specs=[hbm, vmem, vmem, hbm],
+        out_specs=(hbm, vmem, vmem, vmem),
+        scratch_shapes=[
+            v((5, 20, 32, 256), F32),
+            v((5, 18, 32, 256), F32),
+            v((5, 16, 16, 256), F32),
+            v((2, 2, 5, 16, 256), F32),
+            v((2, 2, 5, 32, 256), F32),
+            v((4, 8, 256), F32),
+            v((4, 8, 256), F32),
+            v((128, 256), F32),
+            v((2048, 128), F32),
+            v((1024, 256), F32),
+            v((1024, 256), BF16),
+            v((1024, 256), BF16),
+            v((64, 256), F32),
+            v((32, 2, 256), F32),
+            v((32, 2, 256), F32),
+            v((32, 2, 128), F32),
+            v((32, 2, 128), F32),
+            v((16, 1024), F32),
+            v((32, 8, 384), F32),
+            v((32, 8, 384), F32),
+            v((8, 384), F32),
+            v((4, 8, 384), F32),
+            v((8, 384), F32),
+            v((32, 8, 384), F32),
+            v((2, 256), F32),
+            v((32, 2, 256), F32),
+            v((2, 256), F32),
+            v((4, 2, 256), F32),
+            v((16, 16), F32),
+            v((32, 16, 16), F32),
+            v((16, 16), F32),
+            v((4, 16, 16), F32),
+            pltpu.SemaphoreType.DMA,
+            pltpu.SemaphoreType.DMA,
+            pltpu.SemaphoreType.DMA,
+            pltpu.SemaphoreType.DMA((8,)),
+            pltpu.SemaphoreType.DMA((8,)),
+            pltpu.SemaphoreType.DMA((9,)),
+            pltpu.SemaphoreType.DMA((9,)),
+        ],
+        compiler_params=pltpu.CompilerParams(
+            collective_id=0, has_side_effects=True, vmem_limit_bytes=48 * 1024 * 1024
+        ),
+    )(fields, profiles, earlier, basis_view)
+
+
 def on_device(fields, courant, shear_rate, gradient, earlier, basis_modes, core_matrix):
-    basis_rows = basis_modes.reshape(-1, basis_modes.shape[-1])
-    rows_total = jnp.float32(basis_rows.shape[0] * lax.axis_size("gx") * lax.axis_size("gz"))
-    width_z = fields.shape[2] // 4
-    height = fields.shape[3] // 4
-    buffered = earlier.reshape(earlier.shape[0], earlier.shape[1], width_z, height)
-    halfway = advance_with_rim(fields, courant, shear_rate, gradient)
-    snap_first = coarsen(halfway[0])[None]
-    finished = advance_with_rim(halfway, courant, shear_rate, gradient)
-    snap_second = coarsen(finished[0])[None]
-    snapshots = lax.all_to_all(
-        jnp.concatenate([buffered, snap_first, snap_second], axis=0),
-        "gz",
-        split_axis=3,
-        concat_axis=2,
-        tiled=True,
-    )
-    snapshots = snapshots.reshape(snapshots.shape[0], -1)
-    local_proj = jnp.dot(snapshots, basis_rows, precision=lax.Precision.HIGHEST)
-    c_one = lax.psum(local_proj, ("gx", "gz")) / rows_total
-    p_one = snapshots - jnp.dot(c_one, basis_rows.T, precision=lax.Precision.HIGHEST)
-    local_cross = jnp.dot(p_one, basis_rows, precision=lax.Precision.HIGHEST)
-    c_two = lax.psum(local_cross, ("gx", "gz")) / rows_total
-    residual = p_one - jnp.dot(c_two, basis_rows.T, precision=lax.Precision.HIGHEST)
-    local_gram = jnp.dot(residual, residual.T, precision=lax.Precision.HIGHEST)
-    gram_total = lax.psum(local_gram, ("gx", "gz")) / rows_total
-    coeffs = c_one + c_two
-    ordered = residual.reshape(16, 4, 32, 4, 2).transpose(0, 3, 1, 4, 2).reshape(16, 1024)
-    view, new_core = tail(core_matrix, coeffs, gram_total, ordered, view_of(basis_modes))
-    return (finished, basis_of(view), new_core)
+    sizes = (lax.axis_size("gx"), lax.axis_size("gz"))
+    view = view_of(basis_modes)
+    profiles = jnp.stack([courant, shear_rate, gradient])
+    finished, coeffs, gram, resid = front(sizes, fields, profiles, earlier, view)
+    finished, new_view, new_core = tail(core_matrix, coeffs, gram, resid, view, finished)
+    return (finished, basis_of(new_view), new_core)
 
 
 def solution(mesh):

time: 449 us -> 80.2 us (0.18); the launches traced: 442 us -> 80 us
  blocking collectives: 193 us -> 0 us
  local copies, waits for them, and re-layouts: 156 us -> 3.36 us
  Pallas kernels: 15.6 us -> 75.2 us
  other arithmetic: 47 us -> 0.72 us
  starting transfers between devices: 24.5 us -> 0 us
    psum x3 -> x0, blocking collectives: 193 us -> none  [the longest x1 66.6 us: on_device(): c_one = lax.psum(local_proj, ('gx', 'gz')) / rows_total]
    mul x13 -> x0, local copies, waits for them, and re-layouts: 74.3 us -> none  [the longest x4 25.3 us: advance(): press_coef * 0.5 * (x_upper[3] - x_lower[3])]
    pallas_call x1 -> x2, Pallas kernels: 15.6 us -> 75.2 us  [the longest x1 59.6 us: front(): pl.pallas_call(functools.partial(front_kernel, sizes), out_shape=(jax.Sha...]
    squeeze x3 -> x0, local copies, waits for them, and re-layouts: 32.5 us -> none  [the longest x1 10.9 us: advance(): upwind[1]]
    reduce_sum x1 -> x0, other arithmetic: 28.2 us -> none  [coarsen(): return values.reshape(values.shape[0] // 4, 4, values.shape[1] // 4, 4, v...]
    ppermute x8 -> x0, starting transfers between devices: 20.6 us -> none  [the longest x4 14.4 us: extended(): lax.ppermute(head, axis, [((i + 1) % count, i) for i in range(count)])]
    sub x3 -> x0, local copies, waits for them, and re-layouts: 13 us -> none  [the longest x2 12.7 us: advance(): centre[0] - upwind[0] - shear_rate * centre[1]]
    slice x9 -> x0, local copies, waits for them, and re-layouts: 11.1 us -> none  [the longest x2 4.02 us: advance(): y_lower = jnp.pad(centre[..., :-1], ((0, 0), (0, 0), (0, 0), (1, 0)))]
  transfers between devices with their start and end apart: 9 -> 0, of which waited for: 2 -> 0; matrix products, arithmetic and copies ran while one was open for 25% -> 0% of each run, Pallas kernels for 0% -> 0%
where the time goes in v2:
time: 80.2 us; the launch traced here: 80 us
  Pallas kernels  75.2 us (94%)
  local copies, waits for them, and re-layouts  3.36 us (4%)
    pallas_call x1, Pallas kernels, front(): pl.pallas_call(functools.partial(front_kernel, sizes), out_shape=(jax.Sha...  59.6 us
    pallas_call x1, Pallas kernels, tail(): pl.pallas_call(tail_kernel, out_shape=(jax.ShapeDtypeStruct(fields.shape,...  15.7 us
    unnamed x8, local copies, waits for them, and re-layouts  3.36 us

profile of v2, /device:TPU:1, one launch (start us, length us, event | category | flops | bytes accessed | tf_op | source)
XLA Modules:
  0.0 80.0 jit_solution(193886174874802364)
XLA Ops:
  0.6 0.7 pad_maximum_fusion.profiles_ref
  1.4 0.0 copy-start
  1.4 1.2 %copy-done = f32[4,128,2,256]{3,2,1,0:T(2,128)S(1)} copy-done((f32[4,128,2,256]{3,2,1,0:T(2,128)S(1)}, f32[4,128,2,256]{3,2,1,0:T(2,128)}, u32[]{:S(2)}) %copy-start) | copy-done | bytes 1048600
  2.6 0.0 copy-start.1
  2.6 1.3 %copy-done.1 = f32[5,16,16,256]{3,2,1,0:T(8,128)S(1)} copy-done((f32[5,16,16,256]{3,2,1,0:T(8,128)S(1)}, f32[5,16,16,256]{3,2,1,0:T(8,128)}, u32[]{:S(2)}) %copy-start.1) | copy-done | bytes 1310744
  3.9 0.0 copy-start.3
  3.9 0.8 %copy-done.3 = f32[14,4,256]{2,1,0:T(4,128)S(1)} copy-done((f32[14,4,256]{2,1,0:T(4,128)S(1)}, f32[14,4,256]{2,1,0:T(4,128)}, u32[]{:S(2)}) %copy-start.3) | copy-done | bytes 57368
  4.7 0.0 copy-start.2
  4.7 59.6 %shard_map.94 = (f32[5,16,16,256]{3,2,1,0:T(8,128)S(1)}, f32[16,256]{1,0:T(8,128)S(1)}, f32[16,16]{1,0:T(8,128)S(1)}, f32[16,1024]{1,0:T(8,128)S(1)}) custom-call(f32[5,16,16,256]{3,2,1,0:T(8,128)S(1)} %copy-done.1, f32[3,256]{1,0:T(4,128)S(1)} %pad_maximum_fusion.profiles_ref, f32[14,4,256]{2,1,0:T(4,128)S(1)} %copy-done.3, f32[2048,128]{1,0:T(8,128)S(1)} %bitcast.13), custom_call_target="tpu_custom_call" | custom-call | tf_op jit(solution)/shard_map/pallas_call | solution.py:540
  64.3 0.0 copy-done.2
  64.3 15.7 %shard_map.95 = (f32[5,16,16,256]{3,2,1,0:T(8,128)}, f32[2048,128]{1,0:T(8,128)}, f32[256,256]{1,0:T(8,128)}) custom-call(f32[256,256]{1,0:T(8,128)S(1)} %copy-done.2, f32[16,256]{1,0:T(8,128)S(1)} %get-tuple-element.10.coeffs_ref, f32[16,16]{1,0:T(8,128)S(1)} %get-tuple-element.11.gram_ref, f32[16,1024]{1,0:T(8,128)S(1)} %get-tuple-element.12.resid_ref, ...), custom_call_target="tpu_custom_call" | custom-call | tf_op jit(solution)/shard_map/pallas_call | solution.py:191
Async XLA Ops:
  1.4 1.2 %copy-start = (f32[4,128,2,256]{3,2,1,0:T(2,128)S(1)}, f32[4,128,2,256]{3,2,1,0:T(2,128)}, u32[]{:S(2)}) copy-start(f32[4,128,2,256]{3,2,1,0:T(2,128)} %param.12) | copy-start | bytes 3145732
  2.6 1.3 %copy-start.1 = (f32[5,16,16,256]{3,2,1,0:T(8,128)S(1)}, f32[5,16,16,256]{3,2,1,0:T(8,128)}, u32[]{:S(2)}) copy-start(f32[5,16,16,256]{3,2,1,0:T(8,128)} %fields_hbm.1) | copy-start | bytes 3932164
  3.9 0.8 %copy-start.3 = (f32[14,4,256]{2,1,0:T(4,128)S(1)}, f32[14,4,256]{2,1,0:T(4,128)}, u32[]{:S(2)}) copy-start(f32[14,4,256]{2,1,0:T(4,128)} %earlier_ref.1) | copy-start | bytes 172036
  4.7 59.6 %copy-start.2 = (f32[256,256]{1,0:T(8,128)S(1)}, f32[256,256]{1,0:T(8,128)}, u32[]{:S(2)}) copy-start(f32[256,256]{1,0:T(8,128)} %core_ref.1) | copy-start | bytes 786436

commit v3 on v2

--- a/solution.py
+++ b/solution.py
@@ -85,8 +85,10 @@
     col_index = lax.broadcasted_iota(jnp.int32, (count, count), 1)
     left = gram
     right = eye(count)
+    pivots = jnp.zeros((1, count), F32)
     for j in range(count):
         pivot = left[j : j + 1, j : j + 1]
+        pivots = jnp.where(col_index[:1] == j, pivot, pivots)
         scale = lax.rsqrt(pivot)
         scale = scale * (1.5 - 0.5 * pivot * scale * scale)
         column = left[:, j : j + 1] * scale
@@ -96,7 +98,7 @@
         here = row_index == j
         left = jnp.where(below, left - column * row_l, jnp.where(here, row_l, left))
         right = jnp.where(below, right - column * row_r, jnp.where(here, row_r, right))
-    return jnp.where(row_index <= col_index, left, 0.0), right
+    return jnp.where(row_index <= col_index, left, 0.0), right, pivots
 
 
 def product(left_v, left_d, right_v, right_d):
@@ -114,14 +116,15 @@
     return main + jnp.concatenate([top, low], axis=0), out_d
 
 
-def tail_kernel(core_ref, coeffs_ref, gram_ref, resid_ref, basis_hbm, fields_hbm,
-                out_fields, out_basis, out_core, v_ref, d_ref, basis_view, basis_rows, sem, field_sem):
+def tail_kernel(core_ref, coeffs_ref, factor_ref, inverse_ref, resid_ref, basis_hbm, fields_hbm,
+                out_fields, out_basis, out_core, v_ref, d_ref, basis_view, basis_rows, held, sem, field_sem):
     modes = core_ref.shape[0]
     fetch = pltpu.make_async_copy(basis_hbm, basis_view, sem)
     fetch.start()
-    passing = pltpu.make_async_copy(fields_hbm, out_fields, field_sem)
-    passing.start()
-    factor_t, inverse = cholesky(gram_ref[...] + gram_eps * eye(16))
+    taking = pltpu.make_async_copy(fields_hbm, held, field_sem)
+    taking.start()
+    factor_t = factor_ref[...]
+    inverse = inverse_ref[...]
     coeffs = coeffs_ref[...]
     unit = eye(modes)
     unit_d = eye(16)
@@ -155,6 +158,9 @@
     lax.fori_loop(0, SIGN_STEPS, sign_step, 0)
 
     fetch.wait()
+    taking.wait()
+    passing = pltpu.make_async_copy(held, out_fields, field_sem)
+    passing.start()
     take_basis(basis_view, basis_rows)
 
     rot = 0.5 * (unit_v + v_ref[...])
@@ -185,9 +191,9 @@
     passing.wait()
 
 
-def tail(core, coeffs, gram, resid, basis_view, fields):
+def tail(core, coeffs, factor_t, inverse, resid, basis_view, fields):
     vmem = pl.BlockSpec(memory_space=pltpu.VMEM)
-    hbm = pl.BlockSpec(memory_space=pl.ANY)
+    hbm = pl.BlockSpec(memory_space=pltpu.HBM)
     return pl.pallas_call(
         tail_kernel,
         out_shape=(
@@ -195,18 +201,19 @@
             jax.ShapeDtypeStruct((2048, 128), F32),
             jax.ShapeDtypeStruct((256, 256), F32),
         ),
-        in_specs=[vmem, vmem, vmem, vmem, hbm, hbm],
+        in_specs=[vmem, vmem, vmem, vmem, vmem, hbm, hbm],
         out_specs=(hbm, vmem, vmem),
         scratch_shapes=[
             pltpu.VMEM((272, 256), F32),
             pltpu.VMEM((16, 16), F32),
             pltpu.VMEM((2048, 128), F32),
             pltpu.VMEM((1024, 256), F32),
+            pltpu.VMEM(fields.shape, F32),
             pltpu.SemaphoreType.DMA,
             pltpu.SemaphoreType.DMA,
         ],
-        compiler_params=pltpu.CompilerParams(vmem_limit_bytes=32 * 1024 * 1024),
-    )(core, coeffs, gram, resid, basis_view, fields)
+        compiler_params=pltpu.CompilerParams(vmem_limit_bytes=60 * 1024 * 1024),
+    )(core, coeffs, factor_t, inverse, resid, basis_view, fields)
 
 
 def view_of(basis):
@@ -223,6 +230,7 @@
 visc_coef = 0.05
 heat_coef = 0.03
 FIELDS = 5
+least_pivot = 2.0**-7
 
 
 def shifted(values):
@@ -254,44 +262,70 @@
     return new
 
 
-def front_kernel(sizes, fields_hbm, profiles_ref, earlier_ref, basis_hbm,
-                 out_fields, out_coeffs, out_gram, out_resid,
+def front_kernel(sizes, fields_hbm, courant_hbm, shear_hbm, gradient_hbm, earlier_hbm, basis_hbm,
+                 out_fields, out_coeffs, out_factor, out_inverse, out_sound, out_resid,
                  P, H, F, Zs, Zr, Cs, Cr, V, basis_view, basis_rows, basis_h, basis_l,
                  E2, early_send, early_slots, late_send, late_slots, S,
                  sum_send, sum_slots, sum_mid, sum_mid_slots, sum_out, sum_all,
-                 c_send, c_slots, c_mid, c_mid_slots,
-                 g_send, g_slots, g_mid, g_mid_slots,
-                 load_sem, basis_sem, out_sem, halo_send, halo_recv,
+                 c_send, c_other, c_mid, c_slots,
+                 earlier_ref, profile_rows, small_sem, load_sem, basis_sem, out_sem, halo_send, halo_recv,
                  group_send, group_recv):
     nx, nz = sizes
     gx = lax.axis_index("gx")
     gz = lax.axis_index("gz")
     rows_total = 1024.0 * nx * nz
 
+    barrier = pltpu.get_barrier_semaphore()
+    x_beside = (lax.rem(gx + nx - 1, nx), lax.rem(gx + 1, nx))
+    z_beside = (lax.rem(gz + nz - 1, nz), lax.rem(gz + 1, nz))
+
+    def greet(where):
+        pl.semaphore_signal(barrier, inc=1, device_id=where, device_id_type=MESH)
+
+    def greet_z(d, carry):
+        greet((gx, lax.rem(gz + d, nz)))
+        return carry
+
     load = pltpu.make_async_copy(fields_hbm, P.at[:, 2:18, 8:24, :], load_sem)
     load.start()
     fetch = pltpu.make_async_copy(basis_hbm, basis_view, basis_sem)
     fetch.start()
-
-    barrier = pltpu.get_barrier_semaphore()
-
-    def greet_z(d, carry):
-        pl.semaphore_signal(barrier, inc=1, device_id=(gx, lax.rem(gz + d, nz)), device_id_type=MESH)
-        return carry
-
-    lax.fori_loop(1, nz, greet_z, 0)
+    small = [
+        pltpu.make_async_copy(earlier_hbm, earlier_ref, small_sem.at[0]),
+        pltpu.make_async_copy(courant_hbm, profile_rows.at[0], small_sem.at[1]),
+        pltpu.make_async_copy(shear_hbm, profile_rows.at[1], small_sem.at[2]),
+        pltpu.make_async_copy(gradient_hbm, profile_rows.at[2], small_sem.at[3]),
+    ]
+    for copy in small:
+        copy.start()
     for d in range(1, nx):
-        pl.semaphore_signal(barrier, inc=1, device_id=(lax.rem(gx + d, nx), gz), device_id_type=MESH)
-    x_beside = (lax.rem(gx + nx - 1, nx), lax.rem(gx + 1, nx))
-    z_beside = (lax.rem(gz + nz - 1, nz), lax.rem(gz + 1, nz))
+        greet((lax.rem(gx + d, nx), gz))
     for xs in range(2):
         for zs in range(2):
-            pl.semaphore_signal(
-                barrier, inc=1, device_id=(x_beside[xs], z_beside[zs]), device_id_type=MESH
-            )
+            greet((x_beside[xs], z_beside[zs]))
+    lax.fori_loop(1, nz, greet_z, 0)
 
     load.wait()
-    flat = P.reshape(FIELDS * 20 * 32, 256)
+    pl.semaphore_wait(barrier, nz - 1 + nx - 1 + 4)
+
+    halos = []
+
+    def send_halo(source, target, where):
+        place = len(halos)
+        copy = pltpu.make_async_remote_copy(
+            src_ref=source, dst_ref=target, send_sem=halo_send.at[place],
+            recv_sem=halo_recv.at[place], device_id=where, device_id_type=MESH,
+        )
+        copy.start()
+        halos.append(copy)
+
+    for side in range(2):
+        send_halo(
+            P.at[:, 2 + 14 * side : 4 + 14 * side, 8:24, :],
+            P.at[:, 18 - 18 * side : 20 - 18 * side, 8:24, :],
+            (x_beside[side], gz),
+        )
+
     for side in range(2):
         for layer in range(2):
             z = 8 + 14 * side + layer
@@ -304,27 +338,8 @@
             for f in range(FIELDS):
                 Cs[2 * xs + zs, f : f + 1, :] = P[f, 2 + 15 * xs, 8 + 15 * zs : 9 + 15 * zs, :]
 
-    pl.semaphore_wait(barrier, nz - 1 + nx - 1 + 4)
-
-    halos = []
-
-    def send_halo(source, target, where):
-        place = len(halos)
-        copy = pltpu.make_async_remote_copy(
-            src_ref=source, dst_ref=target, send_sem=halo_send.at[place],
-            recv_sem=halo_recv.at[place], device_id=where, device_id_type=MESH,
-        )
-        copy.start()
-        halos.append(copy)
-
     for side in range(2):
         send_halo(Zs.at[side], Zr.at[1 - side, :, :, 8:24, :], (gx, z_beside[side]))
-    for side in range(2):
-        send_halo(
-            fields_hbm.at[:, 14 * side : 14 * side + 2],
-            P.at[:, 18 - 18 * side : 20 - 18 * side, 8:24, :],
-            (x_beside[side], gz),
-        )
     for xs in range(2):
         for zs in range(2):
             send_halo(
@@ -350,10 +365,43 @@
                 recv_sem=group_recv.at[place], device_id=(peer, gz), device_id_type=MESH,
             ).start()
 
+    core = lax.rem(gx, 2)
+    chip = (gx // 2) * nz + gz
+    chips = (nx // 2) * nz
+
+    def send_core(place, source, target):
+        pltpu.make_async_remote_copy(
+            src_ref=source, dst_ref=target, send_sem=group_send.at[place],
+            recv_sem=group_recv.at[place], device_id=(gx + 1 - 2 * core, gz), device_id_type=MESH,
+        ).start()
+
+    def spread_chips(place, source, slots):
+        def body(d, carry):
+            peer = lax.rem(chip + d, chips)
+            where = (2 * (peer // nz) + core, lax.rem(peer, nz))
+            pltpu.make_async_remote_copy(
+                src_ref=source, dst_ref=slots.at[chip], send_sem=group_send.at[place],
+                recv_sem=group_recv.at[place], device_id=where, device_id_type=MESH,
+            ).start()
+            return carry
+
+        lax.fori_loop(1, chips, body, 0)
+
+    def wait_one(sems, place, part):
+        pltpu.make_async_copy(part, part, sems.at[place]).wait()
+
+    def sum_slots_of(slots):
+        terms = [slots[j] for j in range(slots.shape[0])]
+        while len(terms) > 1:
+            terms = [a + b for a, b in zip(terms[::2], terms[1::2])] + terms[len(terms) & ~1 :]
+        return terms[0]
+
     def wait_all(sems, place, slots):
         some = slots.at[pl.ds(0, slots.shape[0] - 1)]
         pltpu.make_async_copy(some, some, sems.at[place]).wait()
 
+    for copy in small:
+        copy.wait()
     E2[...] = jnp.zeros_like(E2)
     for m in range(14):
         for x in range(4):
@@ -376,22 +424,29 @@
         return basis_h[...], basis_l[...]
 
     inner = dot_three(pair(), pair(), TN)
-    sum_send[:, :, 256:] = jnp.zeros((32, 8, 128), F32)
     for i in range(32):
-        sum_send[i, :, :256] = inner[8 * i : 8 * i + 8]
+        sum_send[i, :, :256] = inner[4 * i : 4 * i + 4]
+        sum_send[i, :, 256:384] = inner[128 + 4 * i : 132 + 4 * i, 128:]
 
     wait_all(group_recv, 0, early_slots)
     got = jnp.concatenate([early_slots[:, 0, :], early_slots[:, 1, :]], axis=0).T
     for zx in range(16):
         S[:, zx * 64 : zx * 64 + 64] = got[zx * 16 : zx * 16 + 16]
     c_early = dot_three(halves(S[...]), pair())
-    for m in range(16):
-        for half in range(2):
-            sum_send[2 * m + half, 0:1, 256:] = c_early[m : m + 1, 128 * half : 128 * half + 128]
+    k_early = dot_three(halves(S[...]), halves(S[...]), NT)
+    k_early = jnp.concatenate([k_early, jnp.zeros((16, 112), F32)], axis=1)
+    lane = lax.broadcasted_iota(jnp.int32, (4, 128), 1)
+    for i in range(32):
+        part = c_early[4 * (i // 8) : 4 * (i // 8) + 4, 128 * (i % 8 // 4) : 128 * (i % 8 // 4) + 128]
+        part = part if i % 4 == 0 else pltpu.roll(part, 128 - 32 * (i % 4), 1)
+        if i % 8 == 0:
+            beyond = pltpu.roll(k_early[i // 2 : i // 2 + 4], 32, 1)
+            part = jnp.where(lane < 32, part, beyond)
+        sum_send[i, :, 384:] = part
     spread_z(1, lambda peer: sum_send.at[peer], sum_slots)
     sum_slots[gz] = sum_send[gz]
 
-    profiles = [profiles_ref[k : k + 1, :] for k in range(3)]
+    profiles = [profile_rows[k] for k in range(3)]
     for copy in halos:
         copy.wait_recv()
     for f in range(FIELDS):
@@ -463,12 +518,16 @@
     late_slots[gz] = late_send[gz]
 
     wait_all(group_recv, 1, sum_slots)
-    total = sum_slots[0]
-    for j in range(1, 32):
-        total = total + sum_slots[j]
+    total = sum_slots_of(sum_slots)
     sum_mid[...] = total
     spread_x(3, sum_mid, sum_mid_slots)
     sum_mid_slots[gx] = total
+
+    wait_all(group_recv, 3, sum_mid_slots)
+    total = ((sum_mid_slots[0] + sum_mid_slots[1]) + sum_mid_slots[2]) + sum_mid_slots[3]
+    sum_out[...] = total
+    spread_z(5, lambda peer: sum_out, sum_all)
+    sum_all[gz] = total
 
     wait_all(group_recv, 2, late_slots)
     got = jnp.concatenate([late_slots[:, 0, :], late_slots[:, 1, :]], axis=0).T
@@ -476,66 +535,69 @@
         S[8:16, zx * 64 : zx * 64 + 64] = S[8:16, zx * 64 : zx * 64 + 64] + got[zx * 8 : zx * 8 + 8]
     low = S[8:16, :]
     low = jnp.where(lax.broadcasted_iota(jnp.int32, low.shape, 0) >= 6, low, 0.0)
-    c_late = dot_three(halves(jnp.concatenate([jnp.zeros_like(low), low], axis=0)), pair())[14:16]
-    c_send[...] = c_late
-    spread_z(4, lambda peer: c_send, c_slots)
-    c_slots[gz] = c_late
-
-    wait_all(group_recv, 3, sum_mid_slots)
-    total = ((sum_mid_slots[0] + sum_mid_slots[1]) + sum_mid_slots[2]) + sum_mid_slots[3]
-    sum_out[...] = total
-    spread_z(5, lambda peer: sum_out, sum_all)
-    sum_all[gz] = total
-
-    wait_all(group_recv, 4, c_slots)
-    total = c_slots[0]
-    for j in range(1, 32):
-        total = total + c_slots[j]
-    c_mid[...] = total
-    spread_x(6, c_mid, c_mid_slots)
-    c_mid_slots[gx] = total
+    late = halves(jnp.concatenate([jnp.zeros_like(low), low], axis=0))
+    c_late = dot_three(late, pair())[14:16]
+    k_late = dot_three(late, halves(S[...]), NT)[14:16]
+    late = jnp.concatenate([c_late, k_late, jnp.zeros((2, 112), F32)], axis=1)
+    c_send[...] = late
+    send_core(4, c_send, c_other)
+    wait_one(group_recv, 4, c_other)
+    both = late + c_other[...]
+    c_mid[...] = both
+    spread_chips(6, c_mid, c_slots)
+    c_slots[chip] = both
 
     wait_all(group_recv, 5, sum_all)
-    metric = sum_all[:, :, :256].reshape(256, 256) * (1.0 / rows_total)
-    early_rows = [
-        jnp.concatenate([sum_all[2 * m, 0:1, 256:], sum_all[2 * m + 1, 0:1, 256:]], axis=1)
-        for m in range(14)
-    ]
-    wait_all(group_recv, 6, c_mid_slots)
-    total = ((c_mid_slots[0] + c_mid_slots[1]) + c_mid_slots[2]) + c_mid_slots[3]
-    c_one = jnp.concatenate(early_rows + [total], axis=0) * (1.0 / rows_total)
-    coeffs = c_one + (c_one - dot_high(c_one, metric))
+    every = sum_all[...].reshape(128, 512)
+    cross = every[:, 128:256]
+    metric = jnp.concatenate(
+        [every[:, :256], jnp.concatenate([cross.T, every[:, 256:384]], axis=1)], axis=0
+    ) * (1.0 / rows_total)
+    early = []
+    for block in range(4):
+        row = [every[4 * (8 * block + i) : 4 * (8 * block + i) + 4, 384:416] for i in range(8)]
+        row.append(every[32 * block : 32 * block + 4, 416:432])
+        row.append(jnp.zeros((4, 112), F32))
+        early.append(jnp.concatenate(row, axis=1))
+    early = jnp.concatenate(early, axis=0)
+    wait_all(group_recv, 6, c_slots)
+    total = jnp.concatenate([early[:14], sum_slots_of(c_slots)], axis=0) * (1.0 / rows_total)
+    c_one = total[:, :256]
+    gram = total[:, 256:272]
+    low_row = lax.broadcasted_iota(jnp.int32, (16, 16), 0) >= 14
+    low_col = lax.broadcasted_iota(jnp.int32, (16, 16), 1) >= 14
+    below = jnp.where(low_row, gram, 0.0)
+    size = jnp.where(low_col & ~low_row, below.T, gram)
+    c_metric = dot_high(c_one, metric)
+    coeffs = 2.0 * c_one - c_metric
     out_coeffs[...] = coeffs
-    resid = S[...] - dot_three(halves(coeffs), pair(), NT)
-    out_resid[...] = resid
-    gram = dot_high(resid, resid, NT) * (1.0 / rows_total)
-    g_send[...] = gram
-    spread_z(7, lambda peer: g_send, g_slots)
-    g_slots[gz] = gram
-    wait_all(group_recv, 7, g_slots)
-    total = g_slots[0]
-    for j in range(1, 32):
-        total = total + g_slots[j]
-    g_mid[...] = total
-    spread_x(8, g_mid, g_mid_slots)
-    g_mid_slots[gx] = total
-    wait_all(group_recv, 8, g_mid_slots)
-    out_gram[...] = ((g_mid_slots[0] + g_mid_slots[1]) + g_mid_slots[2]) + g_mid_slots[3]
+    beyond = 2.0 * c_metric - dot_high(c_metric, metric) - c_one
+    gram = size + dot_high(beyond, coeffs, NT) - dot_high(coeffs, c_one, NT)
+    factor_t, inverse, pivots = cholesky(gram + gram_eps * eye(16))
+    out_factor[...] = factor_t
+    out_inverse[...] = inverse
+    diagonal = eye(16) > 0.0
+    scale = jnp.sum(jnp.where(diagonal, size, 0.0), axis=0, keepdims=True)
+    sound = jnp.where(pivots > least_pivot * scale, 1, 0)
+    out_sound[0, 0] = jnp.min(sound)
+    out_resid[...] = S[...] - dot_three(halves(coeffs), pair(), NT)
 
     for copy in halos:
         copy.wait_send()
-    for place, slots in enumerate([
-        early_slots, sum_slots, late_slots, sum_mid_slots, c_slots, sum_all, c_mid_slots,
-        g_slots, g_mid_slots,
-    ]):
+    for place, slots in (
+        (0, early_slots), (1, sum_slots), (2, late_slots), (3, sum_mid_slots), (5, sum_all),
+        (6, c_slots),
+    ):
         wait_all(group_send, place, slots)
+    wait_one(group_send, 4, c_other)
     store.wait()
 
 
 def front(sizes, fields, profiles, earlier, basis_view):
     nx, nz = sizes
     vmem = pl.BlockSpec(memory_space=pltpu.VMEM)
-    hbm = pl.BlockSpec(memory_space=pl.ANY)
+    hbm = pl.BlockSpec(memory_space=pltpu.HBM)
+    smem = pl.BlockSpec(memory_space=pltpu.SMEM)
     v = pltpu.VMEM
     return pl.pallas_call(
         functools.partial(front_kernel, sizes),
@@ -543,10 +605,12 @@
             jax.ShapeDtypeStruct(fields.shape, F32),
             jax.ShapeDtypeStruct((16, 256), F32),
             jax.ShapeDtypeStruct((16, 16), F32),
+            jax.ShapeDtypeStruct((16, 16), F32),
+            jax.ShapeDtypeStruct((1, 1), jnp.int32),
             jax.ShapeDtypeStruct((16, 1024), F32),
         ),
-        in_specs=[hbm, vmem, vmem, hbm],
-        out_specs=(hbm, vmem, vmem, vmem),
+        in_specs=[hbm] * 6,
+        out_specs=(hbm, vmem, vmem, vmem, smem, vmem),
         scratch_shapes=[
             v((5, 20, 32, 256), F32),
             v((5, 18, 32, 256), F32),
@@ -566,40 +630,57 @@
             v((32, 2, 128), F32),
             v((32, 2, 128), F32),
             v((16, 1024), F32),
-            v((32, 8, 384), F32),
-            v((32, 8, 384), F32),
-            v((8, 384), F32),
-            v((4, 8, 384), F32),
-            v((8, 384), F32),
-            v((32, 8, 384), F32),
-            v((2, 256), F32),
-            v((32, 2, 256), F32),
-            v((2, 256), F32),
-            v((4, 2, 256), F32),
-            v((16, 16), F32),
-            v((32, 16, 16), F32),
-            v((16, 16), F32),
-            v((4, 16, 16), F32),
+            v((32, 4, 512), F32),
+            v((32, 4, 512), F32),
+            v((4, 512), F32),
+            v((4, 4, 512), F32),
+            v((4, 512), F32),
+            v((32, 4, 512), F32),
+            v((2, 384), F32),
+            v((2, 384), F32),
+            v((2, 384), F32),
+            v((64, 2, 384), F32),
+            v((14, 4, 256), F32),
+            v((3, 1, 256), F32),
+            pltpu.SemaphoreType.DMA((4,)),
             pltpu.SemaphoreType.DMA,
             pltpu.SemaphoreType.DMA,
             pltpu.SemaphoreType.DMA,
             pltpu.SemaphoreType.DMA((8,)),
             pltpu.SemaphoreType.DMA((8,)),
-            pltpu.SemaphoreType.DMA((9,)),
-            pltpu.SemaphoreType.DMA((9,)),
+            pltpu.SemaphoreType.DMA((7,)),
+            pltpu.SemaphoreType.DMA((7,)),
         ],
         compiler_params=pltpu.CompilerParams(
-            collective_id=0, has_side_effects=True, vmem_limit_bytes=48 * 1024 * 1024
+            collective_id=0, has_side_effects=True, vmem_limit_bytes=62 * 1024 * 1024
         ),
-    )(fields, profiles, earlier, basis_view)
+    )(fields, *profiles, earlier, basis_view)
+
+
+def direct_factor(resid):
+    rows_total = 1024.0 * lax.axis_size("gx") * lax.axis_size("gz")
+    gram = lax.psum(jnp.dot(resid, resid.T, precision=HIGH), ("gx", "gz")) / rows_total
+    identity = jnp.eye(16, dtype=F32)
+    factor = jnp.linalg.cholesky(gram + gram_eps * identity)
+    return factor.T, jax.scipy.linalg.solve_triangular(factor, identity, lower=True)
 
 
 def on_device(fields, courant, shear_rate, gradient, earlier, basis_modes, core_matrix):
     sizes = (lax.axis_size("gx"), lax.axis_size("gz"))
     view = view_of(basis_modes)
-    profiles = jnp.stack([courant, shear_rate, gradient])
-    finished, coeffs, gram, resid = front(sizes, fields, profiles, earlier, view)
-    finished, new_view, new_core = tail(core_matrix, coeffs, gram, resid, view, finished)
+    profiles = [p.reshape(1, -1) for p in (courant, shear_rate, gradient)]
+    finished, coeffs, factor_t, inverse, sound, resid = front(
+        sizes, fields, profiles, earlier, view
+    )
+    factor_t, inverse = lax.cond(
+        sound[0, 0] > 0,
+        lambda resid, factor_t, inverse: (factor_t, inverse),
+        lambda resid, factor_t, inverse: direct_factor(resid),
+        resid, factor_t, inverse,
+    )
+    finished, new_view, new_core = tail(
+        core_matrix, coeffs, factor_t, inverse, resid, view, finished
+    )
     return (finished, basis_of(new_view), new_core)
 
 

time: 80.2 us -> 65.5 us (0.82)
  Pallas kernels: 75.2 us -> 64 us
  local copies, waits for them, and re-layouts: 3.36 us -> 0 us
    pallas_call x1, Pallas kernels: 59.6 us -> 48.6 us  [front(): pl.pallas_call(functools.partial(front_kernel, sizes), out_shape=(jax.Sha...]
    unnamed x8 -> x0, local copies, waits for them, and re-layouts: 3.36 us -> none
where the time goes in v3:
time: 65.5 us; the launch traced here: 65.3 us
  Pallas kernels  64 us (98%)
  between operations  1.27 us (2%)
    pallas_call x1, Pallas kernels, front(): pl.pallas_call(functools.partial(front_kernel, sizes), out_shape=(jax.Sha...  48.6 us
    pallas_call x1, Pallas kernels, tail(): pl.pallas_call(tail_kernel, out_shape=(jax.ShapeDtypeStruct(fields.shape,...  15.4 us

profile of v3, /device:TPU:1, one launch (start us, length us, event | category | flops | bytes accessed | tf_op | source)
XLA Modules:
  0.0 65.3 jit_solution(15984411168686254214)
XLA Ops:
  0.6 48.6 %shard_map.94 = (f32[5,16,16,256]{3,2,1,0:T(8,128)}, f32[16,256]{1,0:T(8,128)}, f32[16,16]{1,0:T(8,128)S(1)}, f32[16,16]{1,0:T(8,128)S(1)}, s32[1,1]{1,0:T(1,128)}, /*index=5*/f32[16,1024]{1,0:T(8,128)S(1)}) custom-call(f32[5,16,16,256]{3,2,1,0:T(8,128)} %fields_hbm.1, f32[1,256]{1,0:T(1,128)} %bitcast.29, f32[1,256]{1,0:T(1,128)} %bitcast.30, ...), custom_call_target="tpu_custom_call" | custom-call | tf_op jit(solution)/shard_map/pallas_call | solution.py:602
  49.9 15.4 %shard_map.95 = (f32[5,16,16,256]{3,2,1,0:T(8,128)}, f32[2048,128]{1,0:T(8,128)}, f32[256,256]{1,0:T(8,128)}) custom-call(f32[256,256]{1,0:T(8,128)} %core_ref.1, f32[16,256]{1,0:T(8,128)} %get-tuple-element.19.coeffs_ref, f32[16,16]{1,0:T(8,128)S(1)} %get-tuple-element.32.factor_ref, f32[16,16]{1,0:T(8,128)S(1)} %get-tuple-element.25.inverse_ref, ...), custom_call_target="tpu_custom_call" | custom-call | tf_op jit(solution)/shard_map/pallas_call | solution.py:197
  (1 shorter events, 0.0 us)

commit v4 on v3

--- a/solution.py
+++ b/solution.py
@@ -101,19 +101,29 @@
     return jnp.where(row_index <= col_index, left, 0.0), right, pivots
 
 
-def product(left_v, left_d, right_v, right_d):
-    modes = left_v.shape[1]
-    lv = halves(left_v)
-    rv = halves(right_v)
-    ra = (rv[0][:modes], rv[1][:modes])
-    lb = (lv[0][modes:], lv[1][modes:])
-    rb = (rv[0][modes:], rv[1][modes:])
-    main = dot_three(lv, ra)
-    right48 = tripled_right(rb)
-    top = dot(tripled_left(lb), right48, TN)
-    low = dot(tripled_left(halves(left_d)), right48, TN)
-    out_d = dot_three(lb, rb, NT) + dot_high(left_d, right_d)
-    return main + jnp.concatenate([top, low], axis=0), out_d
+def wide_left(v, d):
+    modes = v.shape[1]
+    vh, vl = halves(v)
+    dh, dl = halves(d)
+    bh, bl = vh[modes:].astype(F32), vl[modes:].astype(F32)
+    turned = jnp.concatenate([bh, bh, bl], axis=0).T.astype(BF16)
+    edge = jnp.concatenate([turned, jnp.concatenate([dh, dh, dl], axis=1)], axis=0)
+    return vh, vl, edge, jnp.concatenate([vh[modes:], vh[modes:], vl[modes:], edge[modes:]], axis=1)
+
+
+def product(left, right_v, right_d):
+    modes = right_v.shape[1]
+    rh, rl = halves(right_v)
+    dh, dl = halves(right_d)
+    ah, bh = rh[:modes], rh[modes:]
+    al, bl = rl[:modes], rl[modes:]
+    stacked = jnp.concatenate([ah, al, ah, bh, bl, bh], axis=0)
+    low = jnp.concatenate([bh, bl, bh, dh, dl, dh], axis=1)
+    vh, vl, edge, wide = left
+    thin = jnp.concatenate([bh, bl, bh], axis=0)
+    top = (dot(vh[:modes], ah) + dot(vh[:modes], al)) + (dot(vl[:modes], ah) + dot(edge[:modes], thin))
+    bottom = dot(wide, jnp.concatenate([ah, al, ah, thin], axis=0))
+    return jnp.concatenate([top, bottom], axis=0), dot(wide, low, NT)
 
 
 def tail_kernel(core_ref, coeffs_ref, factor_ref, inverse_ref, resid_ref, basis_hbm, fields_hbm,
@@ -128,7 +138,8 @@
     coeffs = coeffs_ref[...]
     unit = eye(modes)
     unit_d = eye(16)
-    corr_a = core_ref[...] + dot_high(coeffs, coeffs, TN)
+    parts = halves(coeffs)
+    corr_a = core_ref[...] + dot(tripled_left(parts), tripled_right(parts), TN)
     corr_b = dot_high(factor_t, coeffs)
     corr_d = dot_high(factor_t, factor_t, NT)
     shift_a = corr_a - unit
@@ -147,9 +158,10 @@
     def sign_step(step, carry):
         v = v_ref[...]
         d = d_ref[...]
-        square_v, square_d = product(v, d, v, d)
+        left = wide_left(v, d)
+        square_v, square_d = product(left, v, d)
         next_v, next_d = product(
-            v, d, 1.5 * unit_v - 0.5 * square_v, 1.5 * unit_d - 0.5 * square_d
+            left, 1.5 * unit_v - 0.5 * square_v, 1.5 * unit_d - 0.5 * square_d
         )
         v_ref[...] = next_v
         d_ref[...] = next_d
@@ -164,10 +176,16 @@
     take_basis(basis_view, basis_rows)
 
     rot = 0.5 * (unit_v + v_ref[...])
-    for _ in range(POLAR_STEPS):
-        rh, rl = halves(rot)
-        inner = dot_three((rh, rl), (rh, rl), TN)
-        rot = 1.5 * rot - 0.5 * dot_three((rh, rl), halves(inner))
+    pair = halves(rot)
+    top = (pair[0][:modes], pair[1][:modes])
+    low = (pair[0][modes:], pair[1][modes:])
+    inner = dot_three(top, top) + dot(tripled_left(low), tripled_right(low), TN)
+    for step in range(POLAR_STEPS):
+        factor = 1.5 * unit - 0.5 * inner
+        fp = halves(factor)
+        rot = dot_three(halves(rot), fp)
+        if step < POLAR_STEPS - 1:
+            inner = dot_three(halves(dot_three(halves(inner), fp)), fp)
     rp = halves(rot)
     corr_v = jnp.concatenate([corr_a, corr_b], axis=0)
     moved = dot_three(halves(corr_v), (rp[0][:modes], rp[1][:modes]))
@@ -266,7 +284,8 @@
                  out_fields, out_coeffs, out_factor, out_inverse, out_sound, out_resid,
                  P, H, F, Zs, Zr, Cs, Cr, V, basis_view, basis_rows, basis_h, basis_l,
                  E2, early_send, early_slots, late_send, late_slots, S,
-                 sum_send, sum_slots, sum_mid, sum_mid_slots, sum_out, sum_all,
+                 g_send, g_slots, g_mid, g_mid_slots, g_part, g_parts, g_whole, g_all,
+                 e_send, e_slots, e_mid, e_mid_slots, e_part, e_all,
                  c_send, c_other, c_mid, c_slots,
                  earlier_ref, profile_rows, small_sem, load_sem, basis_sem, out_sem, halo_send, halo_recv,
                  group_send, group_recv):
@@ -303,102 +322,9 @@
     for xs in range(2):
         for zs in range(2):
             greet((x_beside[xs], z_beside[zs]))
+    for d in range(1, nx):
+        greet((lax.rem(gx + d, nx), gz + 1 - 2 * lax.rem(gz, 2)))
     lax.fori_loop(1, nz, greet_z, 0)
-
-    load.wait()
-    pl.semaphore_wait(barrier, nz - 1 + nx - 1 + 4)
-
-    halos = []
-
-    def send_halo(source, target, where):
-        place = len(halos)
-        copy = pltpu.make_async_remote_copy(
-            src_ref=source, dst_ref=target, send_sem=halo_send.at[place],
-            recv_sem=halo_recv.at[place], device_id=where, device_id_type=MESH,
-        )
-        copy.start()
-        halos.append(copy)
-
-    for side in range(2):
-        send_halo(
-            P.at[:, 2 + 14 * side : 4 + 14 * side, 8:24, :],
-            P.at[:, 18 - 18 * side : 20 - 18 * side, 8:24, :],
-            (x_beside[side], gz),
-        )
-
-    for side in range(2):
-        for layer in range(2):
-            z = 8 + 14 * side + layer
-            for f in range(FIELDS):
-                for half in range(2):
-                    lanes = pl.ds(128 * half, 128)
-                    Zs[side, layer, f, :, lanes] = P[f, 2:18, z, lanes]
-    for xs in range(2):
-        for zs in range(2):
-            for f in range(FIELDS):
-                Cs[2 * xs + zs, f : f + 1, :] = P[f, 2 + 15 * xs, 8 + 15 * zs : 9 + 15 * zs, :]
-
-    for side in range(2):
-        send_halo(Zs.at[side], Zr.at[1 - side, :, :, 8:24, :], (gx, z_beside[side]))
-    for xs in range(2):
-        for zs in range(2):
-            send_halo(
-                Cs.at[2 * xs + zs], Cr.at[2 * (1 - xs) + 1 - zs], (x_beside[xs], z_beside[zs])
-            )
-
-    def spread_z(place, source, slots):
-        def body(d, carry):
-            peer = lax.rem(gz + d, nz)
-            pltpu.make_async_remote_copy(
-                src_ref=source(peer), dst_ref=slots.at[gz], send_sem=group_send.at[place],
-                recv_sem=group_recv.at[place], device_id=(gx, peer), device_id_type=MESH,
-            ).start()
-            return carry
-
-        lax.fori_loop(1, nz, body, 0)
-
-    def spread_x(place, source, slots):
-        for d in range(1, nx):
-            peer = lax.rem(gx + d, nx)
-            pltpu.make_async_remote_copy(
-                src_ref=source, dst_ref=slots.at[gx], send_sem=group_send.at[place],
-                recv_sem=group_recv.at[place], device_id=(peer, gz), device_id_type=MESH,
-            ).start()
-
-    core = lax.rem(gx, 2)
-    chip = (gx // 2) * nz + gz
-    chips = (nx // 2) * nz
-
-    def send_core(place, source, target):
-        pltpu.make_async_remote_copy(
-            src_ref=source, dst_ref=target, send_sem=group_send.at[place],
-            recv_sem=group_recv.at[place], device_id=(gx + 1 - 2 * core, gz), device_id_type=MESH,
-        ).start()
-
-    def spread_chips(place, source, slots):
-        def body(d, carry):
-            peer = lax.rem(chip + d, chips)
-            where = (2 * (peer // nz) + core, lax.rem(peer, nz))
-            pltpu.make_async_remote_copy(
-                src_ref=source, dst_ref=slots.at[chip], send_sem=group_send.at[place],
-                recv_sem=group_recv.at[place], device_id=where, device_id_type=MESH,
-            ).start()
-            return carry
-
-        lax.fori_loop(1, chips, body, 0)
-
-    def wait_one(sems, place, part):
-        pltpu.make_async_copy(part, part, sems.at[place]).wait()
-
-    def sum_slots_of(slots):
-        terms = [slots[j] for j in range(slots.shape[0])]
-        while len(terms) > 1:
-            terms = [a + b for a, b in zip(terms[::2], terms[1::2])] + terms[len(terms) & ~1 :]
-        return terms[0]
-
-    def wait_all(sems, place, slots):
-        some = slots.at[pl.ds(0, slots.shape[0] - 1)]
-        pltpu.make_async_copy(some, some, sems.at[place]).wait()
 
     for copy in small:
         copy.wait()
@@ -410,6 +336,122 @@
     turned = jnp.concatenate([turned[64 * z : 64 * z + 64] for z in range(4)], axis=1)
     for i in range(32):
         early_send[i] = turned[2 * i : 2 * i + 2]
+    load.wait()
+    pl.semaphore_wait(barrier, nz - 1 + 2 * (nx - 1) + 4)
+
+    halos = []
+
+    def send_halo(source, target, where):
+        place = len(halos)
+        copy = pltpu.make_async_remote_copy(
+            src_ref=source, dst_ref=target, send_sem=halo_send.at[place],
+            recv_sem=halo_recv.at[place], device_id=where, device_id_type=MESH,
+        )
+        copy.start()
+        halos.append(copy)
+
+    for side in range(2):
+        send_halo(
+            P.at[:, 2 + 14 * side : 4 + 14 * side, 8:24, :],
+            P.at[:, 18 - 18 * side : 20 - 18 * side, 8:24, :],
+            (x_beside[side], gz),
+        )
+
+    for side in range(2):
+        for layer in range(2):
+            z = 8 + 14 * side + layer
+            for f in range(FIELDS):
+                for half in range(2):
+                    lanes = pl.ds(128 * half, 128)
+                    Zs[side, layer, f, 8:24, lanes] = P[f, 2:18, z, lanes]
+    for xs in range(2):
+        for zs in range(2):
+            for f in range(FIELDS):
+                Cs[2 * xs + zs, f : f + 1, :] = P[f, 2 + 15 * xs, 8 + 15 * zs : 9 + 15 * zs, :]
+
+    for side in range(2):
+        send_halo(Zs.at[side, :, :, 8:24, :], Zr.at[1 - side, :, :, 8:24, :], (gx, z_beside[side]))
+    for xs in range(2):
+        for zs in range(2):
+            send_halo(
+                Cs.at[2 * xs + zs], Cr.at[2 * (1 - xs) + 1 - zs], (x_beside[xs], z_beside[zs])
+            )
+
+    def spread_z(place, source, slots):
+        def body(d, carry):
+            peer = lax.rem(gz + d, nz)
+            pltpu.make_async_remote_copy(
+                src_ref=source(peer), dst_ref=slots.at[gz], send_sem=group_send.at[place],
+                recv_sem=group_recv.at[place], device_id=(gx, peer), device_id_type=MESH,
+            ).start()
+            return carry
+
+        lax.fori_loop(1, nz, body, 0)
+
+    yz = gz // 2
+    places = nz // 2
+    along = (lax.rem(gz, 2) * (nx // 2) + gx // 2) * 2 + lax.rem(gx, 2)
+    line = 2 * nx
+
+    def spread_yz(place, source, slots):
+        def body(d, carry):
+            peer = lax.rem(yz + d, places)
+            pltpu.make_async_remote_copy(
+                src_ref=source(peer), dst_ref=slots.at[yz], send_sem=group_send.at[place],
+                recv_sem=group_recv.at[place], device_id=(gx, 2 * peer + lax.rem(gz, 2)),
+                device_id_type=MESH,
+            ).start()
+            return carry
+
+        lax.fori_loop(1, places, body, 0)
+
+    def spread_line(place, source, slots):
+        def body(d, carry):
+            peer = lax.rem(along + d, line)
+            where = (lax.rem(peer, nx), 2 * yz + peer // nx)
+            pltpu.make_async_remote_copy(
+                src_ref=source(peer), dst_ref=slots.at[along], send_sem=group_send.at[place],
+                recv_sem=group_recv.at[place], device_id=where, device_id_type=MESH,
+            ).start()
+            return carry
+
+        lax.fori_loop(1, line, body, 0)
+
+    core = lax.rem(gx, 2)
+    chip = (gx // 2) * nz + gz
+    chips = (nx // 2) * nz
+
+    def send_core(place, source, target):
+        pltpu.make_async_remote_copy(
+            src_ref=source, dst_ref=target, send_sem=group_send.at[place],
+            recv_sem=group_recv.at[place], device_id=(gx + 1 - 2 * core, gz), device_id_type=MESH,
+        ).start()
+
+    def spread_chips(place, source, slots):
+        def body(d, carry):
+            peer = lax.rem(chip + d, chips)
+            where = (2 * (peer // nz) + core, lax.rem(peer, nz))
+            pltpu.make_async_remote_copy(
+                src_ref=source, dst_ref=slots.at[chip], send_sem=group_send.at[place],
+                recv_sem=group_recv.at[place], device_id=where, device_id_type=MESH,
+            ).start()
+            return carry
+
+        lax.fori_loop(1, chips, body, 0)
+
+    def wait_one(sems, place, part):
+        pltpu.make_async_copy(part, part, sems.at[place]).wait()
+
+    def sum_slots_of(slots):
+        terms = [slots[j] for j in range(slots.shape[0])]
+        while len(terms) > 1:
+            terms = [a + b for a, b in zip(terms[::2], terms[1::2])] + terms[len(terms) & ~1 :]
+        return terms[0]
+
+    def wait_all(sems, place, slots):
+        some = slots.at[pl.ds(0, slots.shape[0] - 1)]
+        pltpu.make_async_copy(some, some, sems.at[place]).wait()
+
     spread_z(0, lambda peer: early_send.at[peer], early_slots)
     early_slots[gz] = early_send[gz]
 
@@ -424,39 +466,13 @@
         return basis_h[...], basis_l[...]
 
     inner = dot_three(pair(), pair(), TN)
-    for i in range(32):
-        sum_send[i, :, :256] = inner[4 * i : 4 * i + 4]
-        sum_send[i, :, 256:384] = inner[128 + 4 * i : 132 + 4 * i, 128:]
-
-    wait_all(group_recv, 0, early_slots)
-    got = jnp.concatenate([early_slots[:, 0, :], early_slots[:, 1, :]], axis=0).T
-    for zx in range(16):
-        S[:, zx * 64 : zx * 64 + 64] = got[zx * 16 : zx * 16 + 16]
-    c_early = dot_three(halves(S[...]), pair())
-    k_early = dot_three(halves(S[...]), halves(S[...]), NT)
-    k_early = jnp.concatenate([k_early, jnp.zeros((16, 112), F32)], axis=1)
-    lane = lax.broadcasted_iota(jnp.int32, (4, 128), 1)
-    for i in range(32):
-        part = c_early[4 * (i // 8) : 4 * (i // 8) + 4, 128 * (i % 8 // 4) : 128 * (i % 8 // 4) + 128]
-        part = part if i % 4 == 0 else pltpu.roll(part, 128 - 32 * (i % 4), 1)
-        if i % 8 == 0:
-            beyond = pltpu.roll(k_early[i // 2 : i // 2 + 4], 32, 1)
-            part = jnp.where(lane < 32, part, beyond)
-        sum_send[i, :, 384:] = part
-    spread_z(1, lambda peer: sum_send.at[peer], sum_slots)
-    sum_slots[gz] = sum_send[gz]
+    for i in range(16):
+        g_send[i, :, :256] = inner[8 * i : 8 * i + 8]
+        g_send[i, :, 256:] = inner[128 + 8 * i : 136 + 8 * i, 128:]
+    spread_yz(1, lambda peer: g_send.at[peer], g_slots)
+    g_slots[yz] = g_send[yz]
 
     profiles = [profile_rows[k] for k in range(3)]
-    for copy in halos:
-        copy.wait_recv()
-    for f in range(FIELDS):
-        for xs in range(2):
-            row = 7 + 17 * xs
-            for zs in range(2):
-                Zr[zs, 1 - zs, f, row : row + 1, :] = Cr[2 * xs + zs, f : f + 1, :]
-        for zs in range(2):
-            z = 7 + 17 * zs
-            P[f, 1:19, z, :] = Zr[zs, 1 - zs, f, 7:25, :]
 
     def first(i, carry):
         centre = [P[f, i + 1, 8:24, :] for f in range(FIELDS)]
@@ -469,17 +485,54 @@
             H[f, i, 8:24, :] = new[f]
         return carry
 
-    lax.fori_loop(0, 18, first, 0)
+    lax.fori_loop(2, 16, first, 0)
+
+    wait_all(group_recv, 0, early_slots)
+    got = jnp.concatenate([early_slots[:, 0, :], early_slots[:, 1, :]], axis=0).T
+    for zx in range(16):
+        S[:, zx * 64 : zx * 64 + 64] = got[zx * 16 : zx * 16 + 16]
+    snaps = halves(S[...])
+    c_early = dot_three(snaps, pair())
+    k_early = dot_three(snaps, snaps, NT)
+    early = jnp.concatenate([c_early, k_early, jnp.zeros((16, 112), F32)], axis=1)
+    for m in range(16):
+        e_send[m] = early[m : m + 1]
+    spread_yz(8, lambda peer: e_send.at[peer], e_slots)
+    e_slots[yz] = e_send[yz]
+
+    for copy in halos:
+        copy.wait_recv()
+    for f in range(FIELDS):
+        for xs in range(2):
+            row = 7 + 17 * xs
+            x = 1 + 17 * xs
+            for zs in range(2):
+                corner = Cr[2 * xs + zs, f : f + 1, :]
+                Zr[zs, 1 - zs, f, row : row + 1, :] = corner
+                P[f, x, 7 + 17 * zs : 8 + 17 * zs, :] = corner
+                Zs[zs, zs, f, row : row + 1, :] = P[f, x, 8 + 15 * zs : 9 + 15 * zs, :]
+    lax.fori_loop(0, 4, lambda k, carry: first(k + 14 * (k // 2), carry), 0)
     for side in range(2):
-        centre = [Zr[side, 1 - side, f, 8:24, :] for f in range(FIELDS)]
-        xl = [Zr[side, 1 - side, f, 7:23, :] for f in range(FIELDS)]
-        xu = [Zr[side, 1 - side, f, 9:25, :] for f in range(FIELDS)]
-        outer = [Zr[side, side, f, 8:24, :] for f in range(FIELDS)]
-        inside = [Zs[side, side, f, :, :] for f in range(FIELDS)]
-        zl, zu = (outer, inside) if side == 0 else (inside, outer)
-        new = update(centre, xl, xu, zl, zu, profiles)
-        for f in range(FIELDS):
-            H[f, 1:17, 7 + 17 * side, :] = new[f]
+        layers = [Zr.at[side, side], Zr.at[side, 1 - side], Zs.at[side, side], Zs.at[side, 1 - side]]
+        for edge in range(2):
+            outer, mid, inside = layers[edge : edge + 3]
+            centre = [mid[f, 8:24, :] for f in range(FIELDS)]
+            xl = [mid[f, 7:23, :] for f in range(FIELDS)]
+            xu = [mid[f, 9:25, :] for f in range(FIELDS)]
+            out = [outer[f, 8:24, :] for f in range(FIELDS)]
+            within = [inside[f, 8:24, :] for f in range(FIELDS)]
+            zl, zu = (out, within) if side == 0 else (within, out)
+            new = update(centre, xl, xu, zl, zu, profiles)
+            z = 7 + edge if side == 0 else 24 - edge
+            for f in range(FIELDS):
+                H[f, 1:17, z, :] = new[f]
+
+    wait_all(group_recv, 1, g_slots)
+    total = sum_slots_of(g_slots)
+    for r in range(8):
+        g_mid[r] = total[r : r + 1]
+    spread_line(3, lambda peer: g_mid.at[peer], g_mid_slots)
+    g_mid_slots[along] = g_mid[along]
 
     def second(i, carry):
         centre = [H[f, i + 1, 8:24, :] for f in range(FIELDS)]
@@ -506,28 +559,43 @@
     to = lax.broadcasted_iota(jnp.int32, (128, 128), 0)
     of = lax.broadcasted_iota(jnp.int32, (128, 128), 1)
     wanted = ((lax.rem(of, 16) // 4) * 4 + lax.rem(of, 64) // 16) * 8 + 6 + of // 64
-    gathered = dot_high((to == wanted).astype(F32), V[...])
+    place_to = (to == wanted).astype(BF16)
+    sums = halves(V[...])
+    gathered = dot(
+        jnp.concatenate([place_to, place_to], axis=1), jnp.concatenate(sums, axis=0)
+    )
     block = (
         lax.broadcasted_iota(jnp.int32, (64, 256), 0)
         == lax.broadcasted_iota(jnp.int32, (64, 256), 1) // 4
-    ).astype(F32) * (1.0 / 64.0)
-    coarse = dot_high(block, gathered, NT)
+    ).astype(BF16) * BF16(1.0 / 64.0)
+    coarse = dot(
+        jnp.concatenate([block, block], axis=1), jnp.concatenate(halves(gathered), axis=1), NT
+    )
     for i in range(32):
         late_send[i] = coarse[2 * i : 2 * i + 2]
     spread_z(2, lambda peer: late_send.at[peer], late_slots)
     late_slots[gz] = late_send[gz]
 
-    wait_all(group_recv, 1, sum_slots)
-    total = sum_slots_of(sum_slots)
-    sum_mid[...] = total
-    spread_x(3, sum_mid, sum_mid_slots)
-    sum_mid_slots[gx] = total
-
-    wait_all(group_recv, 3, sum_mid_slots)
-    total = ((sum_mid_slots[0] + sum_mid_slots[1]) + sum_mid_slots[2]) + sum_mid_slots[3]
-    sum_out[...] = total
-    spread_z(5, lambda peer: sum_out, sum_all)
-    sum_all[gz] = total
+    wait_all(group_recv, 8, e_slots)
+    e_mid[...] = sum_slots_of(e_slots)
+    spread_line(9, lambda peer: e_mid, e_mid_slots)
+    e_mid_slots[along] = e_mid[...]
+
+    wait_all(group_recv, 3, g_mid_slots)
+    g_part[...] = sum_slots_of(g_mid_slots)
+    spread_line(5, lambda peer: g_part, g_parts)
+    g_parts[along] = g_part[...]
+
+    wait_all(group_recv, 5, g_parts)
+    for r in range(8):
+        g_whole[r : r + 1, :] = g_parts[r]
+    spread_yz(7, lambda peer: g_whole, g_all)
+    g_all[yz] = g_whole[...]
+
+    wait_all(group_recv, 9, e_mid_slots)
+    e_part[...] = sum_slots_of(e_mid_slots)
+    spread_yz(10, lambda peer: e_part, e_all)
+    e_all[yz] = e_part[...]
 
     wait_all(group_recv, 2, late_slots)
     got = jnp.concatenate([late_slots[:, 0, :], late_slots[:, 1, :]], axis=0).T
@@ -536,7 +604,8 @@
     low = S[8:16, :]
     low = jnp.where(lax.broadcasted_iota(jnp.int32, low.shape, 0) >= 6, low, 0.0)
     late = halves(jnp.concatenate([jnp.zeros_like(low), low], axis=0))
-    c_late = dot_three(late, pair())[14:16]
+    both = dot(jnp.concatenate(late, axis=0), basis_h[...])
+    c_late = (both[:16] + both[16:] + dot(late[0], basis_l[...]))[14:16]
     k_late = dot_three(late, halves(S[...]), NT)[14:16]
     late = jnp.concatenate([c_late, k_late, jnp.zeros((2, 112), F32)], axis=1)
     c_send[...] = late
@@ -547,19 +616,16 @@
     spread_chips(6, c_mid, c_slots)
     c_slots[chip] = both
 
-    wait_all(group_recv, 5, sum_all)
-    every = sum_all[...].reshape(128, 512)
+    wait_all(group_recv, 7, g_all)
+    every = g_all[...].reshape(128, 384)
     cross = every[:, 128:256]
     metric = jnp.concatenate(
-        [every[:, :256], jnp.concatenate([cross.T, every[:, 256:384]], axis=1)], axis=0
+        [every[:, :256], jnp.concatenate([cross.T, every[:, 256:]], axis=1)], axis=0
     ) * (1.0 / rows_total)
-    early = []
-    for block in range(4):
-        row = [every[4 * (8 * block + i) : 4 * (8 * block + i) + 4, 384:416] for i in range(8)]
-        row.append(every[32 * block : 32 * block + 4, 416:432])
-        row.append(jnp.zeros((4, 112), F32))
-        early.append(jnp.concatenate(row, axis=1))
-    early = jnp.concatenate(early, axis=0)
+    unit = eye(256)
+    removed = 4.0 * unit - 6.0 * metric + dot_high(dot_high(metric, metric), 4.0 * unit - metric)
+    wait_all(group_recv, 10, e_all)
+    early = e_all[...].reshape(16, 384)
     wait_all(group_recv, 6, c_slots)
     total = jnp.concatenate([early[:14], sum_slots_of(c_slots)], axis=0) * (1.0 / rows_total)
     c_one = total[:, :256]
@@ -568,11 +634,9 @@
     low_col = lax.broadcasted_iota(jnp.int32, (16, 16), 1) >= 14
     below = jnp.where(low_row, gram, 0.0)
     size = jnp.where(low_col & ~low_row, below.T, gram)
-    c_metric = dot_high(c_one, metric)
-    coeffs = 2.0 * c_one - c_metric
+    gram = size - dot_high(dot_high(c_one, removed), c_one, NT)
+    coeffs = 2.0 * c_one - dot_high(c_one, metric)
     out_coeffs[...] = coeffs
-    beyond = 2.0 * c_metric - dot_high(c_metric, metric) - c_one
-    gram = size + dot_high(beyond, coeffs, NT) - dot_high(coeffs, c_one, NT)
     factor_t, inverse, pivots = cholesky(gram + gram_eps * eye(16))
     out_factor[...] = factor_t
     out_inverse[...] = inverse
@@ -585,8 +649,8 @@
     for copy in halos:
         copy.wait_send()
     for place, slots in (
-        (0, early_slots), (1, sum_slots), (2, late_slots), (3, sum_mid_slots), (5, sum_all),
-        (6, c_slots),
+        (0, early_slots), (1, g_slots), (2, late_slots), (3, g_mid_slots), (5, g_parts),
+        (6, c_slots), (7, g_all), (8, e_slots), (9, e_mid_slots), (10, e_all),
     ):
         wait_all(group_send, place, slots)
     wait_one(group_send, 4, c_other)
@@ -615,7 +679,7 @@
             v((5, 20, 32, 256), F32),
             v((5, 18, 32, 256), F32),
             v((5, 16, 16, 256), F32),
-            v((2, 2, 5, 16, 256), F32),
+            v((2, 2, 5, 32, 256), F32),
             v((2, 2, 5, 32, 256), F32),
             v((4, 8, 256), F32),
             v((4, 8, 256), F32),
@@ -630,12 +694,20 @@
             v((32, 2, 128), F32),
             v((32, 2, 128), F32),
             v((16, 1024), F32),
-            v((32, 4, 512), F32),
-            v((32, 4, 512), F32),
-            v((4, 512), F32),
-            v((4, 4, 512), F32),
-            v((4, 512), F32),
-            v((32, 4, 512), F32),
+            v((16, 8, 384), F32),
+            v((16, 8, 384), F32),
+            v((8, 1, 384), F32),
+            v((8, 1, 384), F32),
+            v((1, 384), F32),
+            v((8, 1, 384), F32),
+            v((8, 384), F32),
+            v((16, 8, 384), F32),
+            v((16, 1, 384), F32),
+            v((16, 1, 384), F32),
+            v((1, 384), F32),
+            v((8, 1, 384), F32),
+            v((1, 384), F32),
+            v((16, 1, 384), F32),
             v((2, 384), F32),
             v((2, 384), F32),
             v((2, 384), F32),
@@ -648,8 +720,8 @@
             pltpu.SemaphoreType.DMA,
             pltpu.SemaphoreType.DMA((8,)),
             pltpu.SemaphoreType.DMA((8,)),
-            pltpu.SemaphoreType.DMA((7,)),
-            pltpu.SemaphoreType.DMA((7,)),
+            pltpu.SemaphoreType.DMA((11,)),
+            pltpu.SemaphoreType.DMA((11,)),
         ],
         compiler_params=pltpu.CompilerParams(
             collective_id=0, has_side_effects=True, vmem_limit_bytes=62 * 1024 * 1024

time: 65.5 us -> 62.3 us (0.951)
  Pallas kernels: 64 us -> 60.8 us
    pallas_call x1, Pallas kernels: 48.6 us -> 46.4 us  [front(): pl.pallas_call(functools.partial(front_kernel, sizes), out_shape=(jax.Sha...]
    pallas_call x1, Pallas kernels: 15.4 us -> 14.4 us  [tail(): pl.pallas_call(tail_kernel, out_shape=(jax.ShapeDtypeStruct(fields.shape,...]
where the time goes in v4:
time: 62.3 us; the launch traced here: 62.1 us
  Pallas kernels  60.8 us (98%)
  between operations  1.27 us (2%)
    pallas_call x1, Pallas kernels, front(): pl.pallas_call(functools.partial(front_kernel, sizes), out_shape=(jax.Sha...  46.4 us
    pallas_call x1, Pallas kernels, tail(): pl.pallas_call(tail_kernel, out_shape=(jax.ShapeDtypeStruct(fields.shape,...  14.4 us

profile of v4, /device:TPU:1, one launch (start us, length us, event | category | flops | bytes accessed | tf_op | source)
XLA Modules:
  0.0 62.1 jit_solution(14314282442711327224)
XLA Ops:
  0.6 46.4 %shard_map.94 = (f32[5,16,16,256]{3,2,1,0:T(8,128)}, f32[16,256]{1,0:T(8,128)}, f32[16,16]{1,0:T(8,128)S(1)}, f32[16,16]{1,0:T(8,128)S(1)}, s32[1,1]{1,0:T(1,128)}, /*index=5*/f32[16,1024]{1,0:T(8,128)S(1)}) custom-call(f32[5,16,16,256]{3,2,1,0:T(8,128)} %fields_hbm.1, f32[1,256]{1,0:T(1,128)} %bitcast.29, f32[1,256]{1,0:T(1,128)} %bitcast.30, ...), custom_call_target="tpu_custom_call" | custom-call | tf_op jit(solution)/shard_map/pallas_call | solution.py:666
  47.7 14.4 %shard_map.95 = (f32[5,16,16,256]{3,2,1,0:T(8,128)}, f32[2048,128]{1,0:T(8,128)}, f32[256,256]{1,0:T(8,128)}) custom-call(f32[256,256]{1,0:T(8,128)} %core_ref.1, f32[16,256]{1,0:T(8,128)} %get-tuple-element.19.coeffs_ref, f32[16,16]{1,0:T(8,128)S(1)} %get-tuple-element.32.factor_ref, f32[16,16]{1,0:T(8,128)S(1)} %get-tuple-element.25.inverse_ref, ...), custom_call_target="tpu_custom_call" | custom-call | tf_op jit(solution)/shard_map/pallas_call | solution.py:215
  (1 shorter events, 0.0 us)

commit v5 on v4

--- a/solution.py
+++ b/solution.py
@@ -336,8 +336,23 @@
     turned = jnp.concatenate([turned[64 * z : 64 * z + 64] for z in range(4)], axis=1)
     for i in range(32):
         early_send[i] = turned[2 * i : 2 * i + 2]
+    pl.semaphore_wait(barrier, nz - 1 + 2 * (nx - 1) + 4)
+
+    def spread_z(place, source, slots):
+        def body(d, carry):
+            peer = lax.rem(gz + d, nz)
+            pltpu.make_async_remote_copy(
+                src_ref=source(peer), dst_ref=slots.at[gz], send_sem=group_send.at[place],
+                recv_sem=group_recv.at[place], device_id=(gx, peer), device_id_type=MESH,
+            ).start()
+            return carry
+
+        lax.fori_loop(1, nz, body, 0)
+
+    spread_z(0, lambda peer: early_send.at[peer], early_slots)
+    early_slots[gz] = early_send[gz]
+
     load.wait()
-    pl.semaphore_wait(barrier, nz - 1 + 2 * (nx - 1) + 4)
 
     halos = []
 
@@ -377,17 +392,6 @@
                 Cs.at[2 * xs + zs], Cr.at[2 * (1 - xs) + 1 - zs], (x_beside[xs], z_beside[zs])
             )
 
-    def spread_z(place, source, slots):
-        def body(d, carry):
-            peer = lax.rem(gz + d, nz)
-            pltpu.make_async_remote_copy(
-                src_ref=source(peer), dst_ref=slots.at[gz], send_sem=group_send.at[place],
-                recv_sem=group_recv.at[place], device_id=(gx, peer), device_id_type=MESH,
-            ).start()
-            return carry
-
-        lax.fori_loop(1, nz, body, 0)
-
     yz = gz // 2
     places = nz // 2
     along = (lax.rem(gz, 2) * (nx // 2) + gx // 2) * 2 + lax.rem(gx, 2)
@@ -451,9 +455,6 @@
     def wait_all(sems, place, slots):
         some = slots.at[pl.ds(0, slots.shape[0] - 1)]
         pltpu.make_async_copy(some, some, sems.at[place]).wait()
-
-    spread_z(0, lambda peer: early_send.at[peer], early_slots)
-    early_slots[gz] = early_send[gz]
 
     fetch.wait()
     take_basis(basis_view, basis_rows)

time: 62.3 us -> 60.2 us (0.966)
  Pallas kernels: 60.8 us -> 58.7 us
    pallas_call x1, Pallas kernels: 46.4 us -> 44.4 us  [front(): pl.pallas_call(functools.partial(front_kernel, sizes), out_shape=(jax.Sha...]
where the time goes in v5:
time: 60.2 us; the launch traced here: 60 us
  Pallas kernels  58.7 us (98%)
  between operations  1.27 us (2%)
    pallas_call x1, Pallas kernels, front(): pl.pallas_call(functools.partial(front_kernel, sizes), out_shape=(jax.Sha...  44.4 us
    pallas_call x1, Pallas kernels, tail(): pl.pallas_call(tail_kernel, out_shape=(jax.ShapeDtypeStruct(fields.shape,...  14.4 us

profile of v5, /device:TPU:1, one launch (start us, length us, event | category | flops | bytes accessed | tf_op | source)
XLA Modules:
  0.0 60.0 jit_solution(3419726726163429150)
XLA Ops:
  0.6 44.4 %shard_map.94 = (f32[5,16,16,256]{3,2,1,0:T(8,128)}, f32[16,256]{1,0:T(8,128)}, f32[16,16]{1,0:T(8,128)S(1)}, f32[16,16]{1,0:T(8,128)S(1)}, s32[1,1]{1,0:T(1,128)}, /*index=5*/f32[16,1024]{1,0:T(8,128)S(1)}) custom-call(f32[5,16,16,256]{3,2,1,0:T(8,128)} %fields_hbm.1, f32[1,256]{1,0:T(1,128)} %bitcast.29, f32[1,256]{1,0:T(1,128)} %bitcast.30, ...), custom_call_target="tpu_custom_call" | custom-call | tf_op jit(solution)/shard_map/pallas_call | solution.py:667
  45.6 14.4 %shard_map.95 = (f32[5,16,16,256]{3,2,1,0:T(8,128)}, f32[2048,128]{1,0:T(8,128)}, f32[256,256]{1,0:T(8,128)}) custom-call(f32[256,256]{1,0:T(8,128)} %core_ref.1, f32[16,256]{1,0:T(8,128)} %get-tuple-element.19.coeffs_ref, f32[16,16]{1,0:T(8,128)S(1)} %get-tuple-element.32.factor_ref, f32[16,16]{1,0:T(8,128)S(1)} %get-tuple-element.25.inverse_ref, ...), custom_call_target="tpu_custom_call" | custom-call | tf_op jit(solution)/shard_map/pallas_call | solution.py:215
  (1 shorter events, 0.0 us)

commit v6 on v5

--- a/solution.py
+++ b/solution.py
@@ -259,24 +259,26 @@
     return lower, upper
 
 
-def update(centre, xl, xu, zl, zu, profiles):
+def update(centre, xl, xu, zl, zu, profiles, wanted=range(FIELDS)):
     courant, shear_rate, gradient = profiles
     beside = [shifted(c) for c in centre]
     keep = [1.0 - 6.0 * visc_coef - courant] * 3 + [1.0 - 6.0 * visc_coef]
     keep = keep + [1.0 - 6.0 * heat_coef - courant]
     bring = [visc_coef + courant] * 3 + [visc_coef, heat_coef + courant]
     spread = [visc_coef] * 4 + [heat_coef]
-    new = []
-    for f in range(FIELDS):
+    half_press = 0.5 * press_coef
+    divergence = (xu[0] - xl[0]) + (beside[1][1] - beside[1][0]) + (zu[2] - zl[2])
+    sources = [
+        shear_rate * centre[1] + half_press * (xu[3] - xl[3]),
+        half_press * (beside[3][1] - beside[3][0]),
+        half_press * (zu[3] - zl[3]),
+        0.5 * compress_coef * divergence,
+        gradient * centre[1],
+    ]
+    new = {}
+    for f in wanted:
         around = (xu[f] + zl[f]) + (zu[f] + beside[f][0]) + beside[f][1]
-        new.append(keep[f] * centre[f] + bring[f] * xl[f] + spread[f] * around)
-    half_press = 0.5 * press_coef
-    new[0] = new[0] - shear_rate * centre[1] - half_press * (xu[3] - xl[3])
-    new[1] = new[1] - half_press * (beside[3][1] - beside[3][0])
-    new[2] = new[2] - half_press * (zu[3] - zl[3])
-    divergence = (xu[0] - xl[0]) + (beside[1][1] - beside[1][0]) + (zu[2] - zl[2])
-    new[3] = new[3] - 0.5 * compress_coef * divergence
-    new[4] = new[4] - gradient * centre[1]
+        new[f] = keep[f] * centre[f] + bring[f] * xl[f] + spread[f] * around - sources[f]
     return new
 
 
@@ -475,18 +477,20 @@
 
     profiles = [profile_rows[k] for k in range(3)]
 
-    def first(i, carry):
+    def first(i, wanted=range(FIELDS)):
         centre = [P[f, i + 1, 8:24, :] for f in range(FIELDS)]
         xl = [P[f, i, 8:24, :] for f in range(FIELDS)]
         xu = [P[f, i + 2, 8:24, :] for f in range(FIELDS)]
         zl = [P[f, i + 1, 7:23, :] for f in range(FIELDS)]
         zu = [P[f, i + 1, 9:25, :] for f in range(FIELDS)]
-        new = update(centre, xl, xu, zl, zu, profiles)
-        for f in range(FIELDS):
-            H[f, i, 8:24, :] = new[f]
+        for f, new in update(centre, xl, xu, zl, zu, profiles, wanted).items():
+            H[f, i, 8:24, :] = new
+
+    def first_inside(i, carry):
+        first(i)
         return carry
 
-    lax.fori_loop(2, 16, first, 0)
+    lax.fori_loop(2, 16, first_inside, 0)
 
     wait_all(group_recv, 0, early_slots)
     got = jnp.concatenate([early_slots[:, 0, :], early_slots[:, 1, :]], axis=0).T
@@ -512,21 +516,30 @@
                 Zr[zs, 1 - zs, f, row : row + 1, :] = corner
                 P[f, x, 7 + 17 * zs : 8 + 17 * zs, :] = corner
                 Zs[zs, zs, f, row : row + 1, :] = P[f, x, 8 + 15 * zs : 9 + 15 * zs, :]
-    lax.fori_loop(0, 4, lambda k, carry: first(k + 14 * (k // 2), carry), 0)
-    for side in range(2):
-        layers = [Zr.at[side, side], Zr.at[side, 1 - side], Zs.at[side, side], Zs.at[side, 1 - side]]
-        for edge in range(2):
-            outer, mid, inside = layers[edge : edge + 3]
-            centre = [mid[f, 8:24, :] for f in range(FIELDS)]
-            xl = [mid[f, 7:23, :] for f in range(FIELDS)]
-            xu = [mid[f, 9:25, :] for f in range(FIELDS)]
-            out = [outer[f, 8:24, :] for f in range(FIELDS)]
-            within = [inside[f, 8:24, :] for f in range(FIELDS)]
-            zl, zu = (out, within) if side == 0 else (within, out)
-            new = update(centre, xl, xu, zl, zu, profiles)
-            z = 7 + edge if side == 0 else 24 - edge
-            for f in range(FIELDS):
-                H[f, 1:17, z, :] = new[f]
+
+    def first_edges(wanted):
+        def rows(k, carry):
+            first(k + 14 * (k // 2), wanted)
+            return carry
+
+        lax.fori_loop(0, 4, rows, 0)
+        for side in range(2):
+            layers = [
+                Zr.at[side, side], Zr.at[side, 1 - side], Zs.at[side, side], Zs.at[side, 1 - side]
+            ]
+            for edge in range(2):
+                outer, mid, inside = layers[edge : edge + 3]
+                centre = [mid[f, 8:24, :] for f in range(FIELDS)]
+                xl = [mid[f, 7:23, :] for f in range(FIELDS)]
+                xu = [mid[f, 9:25, :] for f in range(FIELDS)]
+                out = [outer[f, 8:24, :] for f in range(FIELDS)]
+                within = [inside[f, 8:24, :] for f in range(FIELDS)]
+                zl, zu = (out, within) if side == 0 else (within, out)
+                z = 7 + edge if side == 0 else 24 - edge
+                for f, new in update(centre, xl, xu, zl, zu, profiles, wanted).items():
+                    H[f, 1:17, z, :] = new
+
+    first_edges((0, 1, 3))
 
     wait_all(group_recv, 1, g_slots)
     total = sum_slots_of(g_slots)
@@ -535,20 +548,20 @@
     spread_line(3, lambda peer: g_mid.at[peer], g_mid_slots)
     g_mid_slots[along] = g_mid[along]
 
-    def second(i, carry):
-        centre = [H[f, i + 1, 8:24, :] for f in range(FIELDS)]
-        xl = [H[f, i, 8:24, :] for f in range(FIELDS)]
-        xu = [H[f, i + 2, 8:24, :] for f in range(FIELDS)]
-        zl = [H[f, i + 1, 7:23, :] for f in range(FIELDS)]
-        zu = [H[f, i + 1, 9:25, :] for f in range(FIELDS)]
-        new = update(centre, xl, xu, zl, zu, profiles)
-        for f in range(FIELDS):
-            F[f, i, :, :] = new[f]
-        return carry
-
-    lax.fori_loop(0, 16, second, 0)
-    store = pltpu.make_async_copy(F, out_fields, out_sem)
-    store.start()
+    def second(wanted):
+        def row(i, carry):
+            centre = [H[f, i + 1, 8:24, :] for f in range(FIELDS)]
+            xl = [H[f, i, 8:24, :] for f in range(FIELDS)]
+            xu = [H[f, i + 2, 8:24, :] for f in range(FIELDS)]
+            zl = [H[f, i + 1, 7:23, :] for f in range(FIELDS)]
+            zu = [H[f, i + 1, 9:25, :] for f in range(FIELDS)]
+            for f, new in update(centre, xl, xu, zl, zu, profiles, wanted).items():
+                F[f, i, :, :] = new
+            return carry
+
+        lax.fori_loop(0, 16, row, 0)
+
+    second((0,))
 
     for xg in range(4):
         V[16 * xg : 16 * xg + 16, :] = (H[0, 4 * xg + 1, 8:24, :] + H[0, 4 * xg + 2, 8:24, :]) + (
@@ -586,6 +599,11 @@
     g_part[...] = sum_slots_of(g_mid_slots)
     spread_line(5, lambda peer: g_part, g_parts)
     g_parts[along] = g_part[...]
+
+    first_edges((2, 4))
+    second((1, 2, 3, 4))
+    store = pltpu.make_async_copy(F, out_fields, out_sem)
+    store.start()
 
     wait_all(group_recv, 5, g_parts)
     for r in range(8):

time: 60.2 us -> 59.6 us (0.990)
    pallas_call x1, Pallas kernels: 44.4 us -> 43.7 us  [front(): pl.pallas_call(functools.partial(front_kernel, sizes), out_shape=(jax.Sha...]
where the time goes in v6:
time: 59.6 us; the launch traced here: 59.4 us
  Pallas kernels  58.1 us (97%)
  between operations  1.27 us (2%)
    pallas_call x1, Pallas kernels, front(): pl.pallas_call(functools.partial(front_kernel, sizes), out_shape=(jax.Sha...  43.7 us
    pallas_call x1, Pallas kernels, tail(): pl.pallas_call(tail_kernel, out_shape=(jax.ShapeDtypeStruct(fields.shape,...  14.4 us

profile of v6, /device:TPU:1, one launch (start us, length us, event | category | flops | bytes accessed | tf_op | source)
XLA Modules:
  0.0 59.4 jit_solution(8539036706473171325)
XLA Ops:
  0.6 43.7 %shard_map.94 = (f32[5,16,16,256]{3,2,1,0:T(8,128)}, f32[16,256]{1,0:T(8,128)}, f32[16,16]{1,0:T(8,128)S(1)}, f32[16,16]{1,0:T(8,128)S(1)}, s32[1,1]{1,0:T(1,128)}, /*index=5*/f32[16,1024]{1,0:T(8,128)S(1)}) custom-call(f32[5,16,16,256]{3,2,1,0:T(8,128)} %fields_hbm.1, f32[1,256]{1,0:T(1,128)} %bitcast.29, f32[1,256]{1,0:T(1,128)} %bitcast.30, ...), custom_call_target="tpu_custom_call" | custom-call | tf_op jit(solution)/shard_map/pallas_call | solution.py:685
  45.0 14.4 %shard_map.95 = (f32[5,16,16,256]{3,2,1,0:T(8,128)}, f32[2048,128]{1,0:T(8,128)}, f32[256,256]{1,0:T(8,128)}) custom-call(f32[256,256]{1,0:T(8,128)} %core_ref.1, f32[16,256]{1,0:T(8,128)} %get-tuple-element.19.coeffs_ref, f32[16,16]{1,0:T(8,128)S(1)} %get-tuple-element.32.factor_ref, f32[16,16]{1,0:T(8,128)S(1)} %get-tuple-element.25.inverse_ref, ...), custom_call_target="tpu_custom_call" | custom-call | tf_op jit(solution)/shard_map/pallas_call | solution.py:215
  (1 shorter events, 0.0 us)

commit v7 on v6

--- a/solution.py
+++ b/solution.py
@@ -79,16 +79,12 @@
             ]
 
 
-def cholesky(gram):
-    count = gram.shape[0]
-    row_index = lax.broadcasted_iota(jnp.int32, (count, count), 0)
-    col_index = lax.broadcasted_iota(jnp.int32, (count, count), 1)
-    left = gram
-    right = eye(count)
-    pivots = jnp.zeros((1, count), F32)
-    for j in range(count):
+def eliminate(left, right, pivots, columns):
+    row_index = lax.broadcasted_iota(jnp.int32, left.shape, 0)
+    col_index = lax.broadcasted_iota(jnp.int32, pivots.shape, 1)
+    for j in columns:
         pivot = left[j : j + 1, j : j + 1]
-        pivots = jnp.where(col_index[:1] == j, pivot, pivots)
+        pivots = jnp.where(col_index == j, pivot, pivots)
         scale = lax.rsqrt(pivot)
         scale = scale * (1.5 - 0.5 * pivot * scale * scale)
         column = left[:, j : j + 1] * scale
@@ -98,7 +94,7 @@
         here = row_index == j
         left = jnp.where(below, left - column * row_l, jnp.where(here, row_l, left))
         right = jnp.where(below, right - column * row_r, jnp.where(here, row_r, right))
-    return jnp.where(row_index <= col_index, left, 0.0), right, pivots
+    return left, right, pivots
 
 
 def wide_left(v, d):
@@ -126,7 +122,7 @@
     return jnp.concatenate([top, bottom], axis=0), dot(wide, low, NT)
 
 
-def tail_kernel(core_ref, coeffs_ref, factor_ref, inverse_ref, resid_ref, basis_hbm, fields_hbm,
+def tail_kernel(core_ref, coeffs_ref, factor_ref, inverse_ref, snaps_ref, basis_hbm, fields_hbm,
                 out_fields, out_basis, out_core, v_ref, d_ref, basis_view, basis_rows, held, sem, field_sem):
     modes = core_ref.shape[0]
     fetch = pltpu.make_async_copy(basis_hbm, basis_view, sem)
@@ -201,15 +197,15 @@
 
     mix = dot_high(inverse, rot[modes:], TN)
     mix48 = tripled_right(halves(mix))
-    ra = (rp[0][:modes], rp[1][:modes])
+    ra = halves(rot[:modes] - dot(tripled_left(parts), mix48, TN))
     for part in range(4):
         rows = basis_rows[pl.ds(part * 256, 256), :]
-        left = tripled_left(halves(resid_ref[:, part * 256 : part * 256 + 256]))
+        left = tripled_left(halves(snaps_ref[:, part * 256 : part * 256 + 256]))
         give_basis(dot_three(halves(rows), ra) + dot(left, mix48, TN), out_basis, part * 8)
     passing.wait()
 
 
-def tail(core, coeffs, factor_t, inverse, resid, basis_view, fields):
+def tail(core, coeffs, factor_t, inverse, snaps, basis_view, fields):
     vmem = pl.BlockSpec(memory_space=pltpu.VMEM)
     hbm = pl.BlockSpec(memory_space=pltpu.HBM)
     return pl.pallas_call(
@@ -231,7 +227,7 @@
             pltpu.SemaphoreType.DMA,
         ],
         compiler_params=pltpu.CompilerParams(vmem_limit_bytes=60 * 1024 * 1024),
-    )(core, coeffs, factor_t, inverse, resid, basis_view, fields)
+    )(core, coeffs, factor_t, inverse, snaps, basis_view, fields)
 
 
 def view_of(basis):
@@ -283,7 +279,7 @@
 
 
 def front_kernel(sizes, fields_hbm, courant_hbm, shear_hbm, gradient_hbm, earlier_hbm, basis_hbm,
-                 out_fields, out_coeffs, out_factor, out_inverse, out_sound, out_resid,
+                 out_fields, out_coeffs, out_factor, out_inverse, out_sound, out_snaps,
                  P, H, F, Zs, Zr, Cs, Cr, V, basis_view, basis_rows, basis_h, basis_l,
                  E2, early_send, early_slots, late_send, late_slots, S,
                  g_send, g_slots, g_mid, g_mid_slots, g_part, g_parts, g_whole, g_all,
@@ -620,6 +616,7 @@
     got = jnp.concatenate([late_slots[:, 0, :], late_slots[:, 1, :]], axis=0).T
     for zx in range(16):
         S[8:16, zx * 64 : zx * 64 + 64] = S[8:16, zx * 64 : zx * 64 + 64] + got[zx * 8 : zx * 8 + 8]
+    out_snaps[...] = S[...]
     low = S[8:16, :]
     low = jnp.where(lax.broadcasted_iota(jnp.int32, low.shape, 0) >= 6, low, 0.0)
     late = halves(jnp.concatenate([jnp.zeros_like(low), low], axis=0))
@@ -644,26 +641,36 @@
     unit = eye(256)
     removed = 4.0 * unit - 6.0 * metric + dot_high(dot_high(metric, metric), 4.0 * unit - metric)
     wait_all(group_recv, 10, e_all)
-    early = e_all[...].reshape(16, 384)
-    wait_all(group_recv, 6, c_slots)
-    total = jnp.concatenate([early[:14], sum_slots_of(c_slots)], axis=0) * (1.0 / rows_total)
-    c_one = total[:, :256]
-    gram = total[:, 256:272]
+    early = e_all[...].reshape(16, 384) * (1.0 / rows_total)
+    c_early = early[:, :256]
+    identity = eye(16)
+    gram = early[:, 256:272] - dot_high(dot_high(c_early, removed), c_early, NT)
+    left, right, pivots = eliminate(
+        gram + gram_eps * identity, identity, jnp.zeros((1, 16), F32), range(14)
+    )
     low_row = lax.broadcasted_iota(jnp.int32, (16, 16), 0) >= 14
     low_col = lax.broadcasted_iota(jnp.int32, (16, 16), 1) >= 14
-    below = jnp.where(low_row, gram, 0.0)
-    size = jnp.where(low_col & ~low_row, below.T, gram)
-    gram = size - dot_high(dot_high(c_one, removed), c_one, NT)
-    coeffs = 2.0 * c_one - dot_high(c_one, metric)
-    out_coeffs[...] = coeffs
-    factor_t, inverse, pivots = cholesky(gram + gram_eps * eye(16))
-    out_factor[...] = factor_t
-    out_inverse[...] = inverse
-    diagonal = eye(16) > 0.0
-    scale = jnp.sum(jnp.where(diagonal, size, 0.0), axis=0, keepdims=True)
+
+    wait_all(group_recv, 6, c_slots)
+    total = jnp.concatenate([early[:14], sum_slots_of(c_slots) * (1.0 / rows_total)], axis=0)
+    c_one = total[:, :256]
+    size = total[:, 256:272]
+    out_coeffs[...] = 2.0 * c_one - dot_high(c_one, metric)
+    gram = size - dot_high(dot_high(c_one, removed), c_one, NT) + gram_eps * identity
+    across = dot_high(jnp.where(low_row & ~low_col, gram, 0.0), right, NT)
+    corner = jnp.where(low_row & low_col, gram, 0.0) - dot_high(across, across, NT)
+    left, right, pivots = eliminate(
+        jnp.where(low_row, corner, left + across.T), right - dot_high(across, right), pivots,
+        range(14, 16),
+    )
+    upper = lax.broadcasted_iota(jnp.int32, (16, 16), 0) <= lax.broadcasted_iota(
+        jnp.int32, (16, 16), 1
+    )
+    out_factor[...] = jnp.where(upper, left, 0.0)
+    out_inverse[...] = right
+    scale = jnp.sum(jnp.where(identity > 0.0, size, 0.0), axis=0, keepdims=True)
     sound = jnp.where(pivots > least_pivot * scale, 1, 0)
     out_sound[0, 0] = jnp.min(sound)
-    out_resid[...] = S[...] - dot_three(halves(coeffs), pair(), NT)
 
     for copy in halos:
         copy.wait_send()
@@ -748,8 +755,10 @@
     )(fields, *profiles, earlier, basis_view)
 
 
-def direct_factor(resid):
+def direct_factor(snaps, coeffs, basis_modes):
     rows_total = 1024.0 * lax.axis_size("gx") * lax.axis_size("gz")
+    rows = basis_modes.reshape(4, 32, 4, 2, 256).transpose(2, 0, 3, 1, 4).reshape(1024, 256)
+    resid = snaps - jnp.dot(coeffs, rows.T, precision=HIGH)
     gram = lax.psum(jnp.dot(resid, resid.T, precision=HIGH), ("gx", "gz")) / rows_total
     identity = jnp.eye(16, dtype=F32)
     factor = jnp.linalg.cholesky(gram + gram_eps * identity)
@@ -760,17 +769,19 @@
     sizes = (lax.axis_size("gx"), lax.axis_size("gz"))
     view = view_of(basis_modes)
     profiles = [p.reshape(1, -1) for p in (courant, shear_rate, gradient)]
-    finished, coeffs, factor_t, inverse, sound, resid = front(
+    finished, coeffs, factor_t, inverse, sound, snaps = front(
         sizes, fields, profiles, earlier, view
     )
     factor_t, inverse = lax.cond(
         sound[0, 0] > 0,
-        lambda resid, factor_t, inverse: (factor_t, inverse),
-        lambda resid, factor_t, inverse: direct_factor(resid),
-        resid, factor_t, inverse,
+        lambda snaps, coeffs, basis_modes, factor_t, inverse: (factor_t, inverse),
+        lambda snaps, coeffs, basis_modes, factor_t, inverse: direct_factor(
+            snaps, coeffs, basis_modes
+        ),
+        snaps, coeffs, basis_modes, factor_t, inverse,
     )
     finished, new_view, new_core = tail(
-        core_matrix, coeffs, factor_t, inverse, resid, view, finished
+        core_matrix, coeffs, factor_t, inverse, snaps, view, finished
     )
     return (finished, basis_of(new_view), new_core)
 

time: 59.6 us -> 58.7 us (0.985)
  Pallas kernels: 58.1 us -> 57.2 us
    pallas_call x1, Pallas kernels: 43.7 us -> 42.8 us  [front(): pl.pallas_call(functools.partial(front_kernel, sizes), out_shape=(jax.Sha...]
where the time goes in v7:
time: 58.7 us; the launch traced here: 58.5 us
  Pallas kernels  57.2 us (97%)
  between operations  1.29 us (2%)
    pallas_call x1, Pallas kernels, front(): pl.pallas_call(functools.partial(front_kernel, sizes), out_shape=(jax.Sha...  42.8 us
    pallas_call x1, Pallas kernels, tail(): pl.pallas_call(tail_kernel, out_shape=(jax.ShapeDtypeStruct(fields.shape,...  14.4 us

profile of v7, /device:TPU:1, one launch (start us, length us, event | category | flops | bytes accessed | tf_op | source)
XLA Modules:
  0.0 58.5 jit_solution(6959737650333932450)
XLA Ops:
  0.6 0.0 copy-start
  0.6 42.8 %shard_map.94 = (f32[5,16,16,256]{3,2,1,0:T(8,128)}, f32[16,256]{1,0:T(8,128)S(1)}, f32[16,16]{1,0:T(8,128)S(1)}, f32[16,16]{1,0:T(8,128)S(1)}, s32[1,1]{1,0:T(1,128)}, /*index=5*/f32[16,1024]{1,0:T(8,128)S(1)}) custom-call(f32[5,16,16,256]{3,2,1,0:T(8,128)} %fields_hbm.1, f32[1,256]{1,0:T(1,128)} %bitcast.37, f32[1,256]{1,0:T(1,128)} %bitcast.38, ...), custom_call_target="tpu_custom_call" | custom-call | tf_op jit(solution)/shard_map/pallas_call | solution.py:692
  44.0 0.0 copy-done
  44.1 14.4 %shard_map.95 = (f32[5,16,16,256]{3,2,1,0:T(8,128)}, f32[2048,128]{1,0:T(8,128)}, f32[256,256]{1,0:T(8,128)}) custom-call(f32[256,256]{1,0:T(8,128)} %core_ref.1, f32[16,256]{1,0:T(8,128)S(1)} %get-tuple-element.27.coeffs_ref, f32[16,16]{1,0:T(8,128)S(1)} %get-tuple-element.44.factor_ref, f32[16,16]{1,0:T(8,128)S(1)} %get-tuple-element.33.inverse_ref, ...), custom_call_target="tpu_custom_call" | custom-call | tf_op jit(solution)/shard_map/pallas_call | solution.py:211
  (1 shorter events, 0.0 us)
Async XLA Ops:
  0.6 43.4 %copy-start = (f32[4,128,2,256]{3,2,1,0:T(2,128)S(1)}, f32[4,128,2,256]{3,2,1,0:T(2,128)}, u32[]{:S(2)}) copy-start(f32[4,128,2,256]{3,2,1,0:T(2,128)} %param.14) | copy-start | bytes 3145732

commit v8 on v7

--- a/solution.py
+++ b/solution.py
@@ -255,22 +255,34 @@
     return lower, upper
 
 
+class Fields:
+    def __init__(self, read):
+        self.read = read
+        self.known = {}
+
+    def __getitem__(self, f):
+        if f not in self.known:
+            self.known[f] = self.read(f)
+        return self.known[f]
+
+
 def update(centre, xl, xu, zl, zu, profiles, wanted=range(FIELDS)):
     courant, shear_rate, gradient = profiles
-    beside = [shifted(c) for c in centre]
+    beside = Fields(lambda f: shifted(centre[f]))
     keep = [1.0 - 6.0 * visc_coef - courant] * 3 + [1.0 - 6.0 * visc_coef]
     keep = keep + [1.0 - 6.0 * heat_coef - courant]
     bring = [visc_coef + courant] * 3 + [visc_coef, heat_coef + courant]
     spread = [visc_coef] * 4 + [heat_coef]
     half_press = 0.5 * press_coef
-    divergence = (xu[0] - xl[0]) + (beside[1][1] - beside[1][0]) + (zu[2] - zl[2])
-    sources = [
-        shear_rate * centre[1] + half_press * (xu[3] - xl[3]),
-        half_press * (beside[3][1] - beside[3][0]),
-        half_press * (zu[3] - zl[3]),
-        0.5 * compress_coef * divergence,
-        gradient * centre[1],
-    ]
+    sources = Fields(lambda f: (
+        lambda: shear_rate * centre[1] + half_press * (xu[3] - xl[3]),
+        lambda: half_press * (beside[3][1] - beside[3][0]),
+        lambda: half_press * (zu[3] - zl[3]),
+        lambda: 0.5 * compress_coef * (
+            (xu[0] - xl[0]) + (beside[1][1] - beside[1][0]) + (zu[2] - zl[2])
+        ),
+        lambda: gradient * centre[1],
+    )[f]())
     new = {}
     for f in wanted:
         around = (xu[f] + zl[f]) + (zu[f] + beside[f][0]) + beside[f][1]
@@ -363,12 +375,26 @@
         copy.start()
         halos.append(copy)
 
-    for side in range(2):
+    def send_x(side, fields, layers):
+        first_own = 2 + 14 * side + layers[0]
+        first_there = 18 - 18 * side + layers[0]
         send_halo(
-            P.at[:, 2 + 14 * side : 4 + 14 * side, 8:24, :],
-            P.at[:, 18 - 18 * side : 20 - 18 * side, 8:24, :],
+            P.at[fields, first_own : first_own + len(layers), 8:24, :],
+            P.at[fields, first_there : first_there + len(layers), 8:24, :],
             (x_beside[side], gz),
         )
+
+    def send_z(side, layer, fields):
+        send_halo(
+            Zs.at[side, layer, fields, 8:24, :],
+            Zr.at[1 - side, layer, fields, 8:24, :],
+            (gx, z_beside[side]),
+        )
+
+    for side in range(2):
+        send_x(side, pl.ds(0, 1), (0, 1))
+        send_x(side, pl.ds(3, 1), (0, 1))
+        send_x(side, pl.ds(1, 2), (side,))
 
     for side in range(2):
         for layer in range(2):
@@ -383,12 +409,14 @@
                 Cs[2 * xs + zs, f : f + 1, :] = P[f, 2 + 15 * xs, 8 + 15 * zs : 9 + 15 * zs, :]
 
     for side in range(2):
-        send_halo(Zs.at[side, :, :, 8:24, :], Zr.at[1 - side, :, :, 8:24, :], (gx, z_beside[side]))
+        send_z(side, side, pl.ds(0, 4))
+        send_z(side, 1 - side, pl.ds(0, 1))
     for xs in range(2):
         for zs in range(2):
             send_halo(
                 Cs.at[2 * xs + zs], Cr.at[2 * (1 - xs) + 1 - zs], (x_beside[xs], z_beside[zs])
             )
+    urgent = len(halos)
 
     yz = gz // 2
     places = nz // 2
@@ -470,15 +498,20 @@
         g_send[i, :, 256:] = inner[128 + 8 * i : 136 + 8 * i, 128:]
     spread_yz(1, lambda peer: g_send.at[peer], g_slots)
     g_slots[yz] = g_send[yz]
+    for side in range(2):
+        send_x(side, pl.ds(1, 2), (1 - side,))
+        send_x(side, pl.ds(4, 1), (0, 1))
+        send_z(side, side, pl.ds(4, 1))
+        send_z(side, 1 - side, pl.ds(1, 4))
 
     profiles = [profile_rows[k] for k in range(3)]
 
     def first(i, wanted=range(FIELDS)):
-        centre = [P[f, i + 1, 8:24, :] for f in range(FIELDS)]
-        xl = [P[f, i, 8:24, :] for f in range(FIELDS)]
-        xu = [P[f, i + 2, 8:24, :] for f in range(FIELDS)]
-        zl = [P[f, i + 1, 7:23, :] for f in range(FIELDS)]
-        zu = [P[f, i + 1, 9:25, :] for f in range(FIELDS)]
+        centre = Fields(lambda f: P[f, i + 1, 8:24, :])
+        xl = Fields(lambda f: P[f, i, 8:24, :])
+        xu = Fields(lambda f: P[f, i + 2, 8:24, :])
+        zl = Fields(lambda f: P[f, i + 1, 7:23, :])
+        zu = Fields(lambda f: P[f, i + 1, 9:25, :])
         for f, new in update(centre, xl, xu, zl, zu, profiles, wanted).items():
             H[f, i, 8:24, :] = new
 
@@ -501,56 +534,60 @@
     spread_yz(8, lambda peer: e_send.at[peer], e_slots)
     e_slots[yz] = e_send[yz]
 
-    for copy in halos:
+    for copy in halos[:urgent]:
         copy.wait_recv()
-    for f in range(FIELDS):
-        for xs in range(2):
-            row = 7 + 17 * xs
-            x = 1 + 17 * xs
-            for zs in range(2):
-                corner = Cr[2 * xs + zs, f : f + 1, :]
-                Zr[zs, 1 - zs, f, row : row + 1, :] = corner
-                P[f, x, 7 + 17 * zs : 8 + 17 * zs, :] = corner
-                Zs[zs, zs, f, row : row + 1, :] = P[f, x, 8 + 15 * zs : 9 + 15 * zs, :]
-
-    def first_edges(wanted):
-        def rows(k, carry):
-            first(k + 14 * (k // 2), wanted)
+
+    def fill_corners(fields):
+        for f in fields:
+            for xs in range(2):
+                row = 7 + 17 * xs
+                x = 1 + 17 * xs
+                for zs in range(2):
+                    corner = Cr[2 * xs + zs, f : f + 1, :]
+                    Zr[zs, 1 - zs, f, row : row + 1, :] = corner
+                    P[f, x, 7 + 17 * zs : 8 + 17 * zs, :] = corner
+                    Zs[zs, zs, f, row : row + 1, :] = P[f, x, 8 + 15 * zs : 9 + 15 * zs, :]
+
+    def first_edges(outside_x, outside_z, inside):
+        def outside_rows(k, carry):
+            first(17 * k, outside_x)
             return carry
 
-        lax.fori_loop(0, 4, rows, 0)
+        def inside_rows(k, carry):
+            first(1 + 15 * k, inside)
+            return carry
+
+        lax.fori_loop(0, 2, outside_rows, 0)
+        lax.fori_loop(0, 2, inside_rows, 0)
         for side in range(2):
             layers = [
                 Zr.at[side, side], Zr.at[side, 1 - side], Zs.at[side, side], Zs.at[side, 1 - side]
             ]
             for edge in range(2):
-                outer, mid, inside = layers[edge : edge + 3]
-                centre = [mid[f, 8:24, :] for f in range(FIELDS)]
-                xl = [mid[f, 7:23, :] for f in range(FIELDS)]
-                xu = [mid[f, 9:25, :] for f in range(FIELDS)]
-                out = [outer[f, 8:24, :] for f in range(FIELDS)]
-                within = [inside[f, 8:24, :] for f in range(FIELDS)]
-                zl, zu = (out, within) if side == 0 else (within, out)
-                z = 7 + edge if side == 0 else 24 - edge
-                for f, new in update(centre, xl, xu, zl, zu, profiles, wanted).items():
-                    H[f, 1:17, z, :] = new
-
-    first_edges((0, 1, 3))
-
-    wait_all(group_recv, 1, g_slots)
-    total = sum_slots_of(g_slots)
-    for r in range(8):
-        g_mid[r] = total[r : r + 1]
-    spread_line(3, lambda peer: g_mid.at[peer], g_mid_slots)
-    g_mid_slots[along] = g_mid[along]
+                edge_layer(side, edge, layers[edge : edge + 3], (outside_z, inside)[edge])
+
+    def edge_layer(side, edge, layers, wanted):
+        outer, mid, inside = layers
+        centre = Fields(lambda f: mid[f, 8:24, :])
+        xl = Fields(lambda f: mid[f, 7:23, :])
+        xu = Fields(lambda f: mid[f, 9:25, :])
+        out = Fields(lambda f: outer[f, 8:24, :])
+        within = Fields(lambda f: inside[f, 8:24, :])
+        zl, zu = (out, within) if side == 0 else (within, out)
+        z = 7 + edge if side == 0 else 24 - edge
+        for f, new in update(centre, xl, xu, zl, zu, profiles, wanted).items():
+            H[f, 1:17, z, :] = new
+
+    fill_corners(range(4))
+    first_edges((0, 3), (0,), (0, 1, 3))
 
     def second(wanted):
         def row(i, carry):
-            centre = [H[f, i + 1, 8:24, :] for f in range(FIELDS)]
-            xl = [H[f, i, 8:24, :] for f in range(FIELDS)]
-            xu = [H[f, i + 2, 8:24, :] for f in range(FIELDS)]
-            zl = [H[f, i + 1, 7:23, :] for f in range(FIELDS)]
-            zu = [H[f, i + 1, 9:25, :] for f in range(FIELDS)]
+            centre = Fields(lambda f: H[f, i + 1, 8:24, :])
+            xl = Fields(lambda f: H[f, i, 8:24, :])
+            xu = Fields(lambda f: H[f, i + 2, 8:24, :])
+            zl = Fields(lambda f: H[f, i + 1, 7:23, :])
+            zu = Fields(lambda f: H[f, i + 1, 9:25, :])
             for f, new in update(centre, xl, xu, zl, zu, profiles, wanted).items():
                 F[f, i, :, :] = new
             return carry
@@ -586,6 +623,13 @@
     spread_z(2, lambda peer: late_send.at[peer], late_slots)
     late_slots[gz] = late_send[gz]
 
+    wait_all(group_recv, 1, g_slots)
+    total = sum_slots_of(g_slots)
+    for r in range(8):
+        g_mid[r] = total[r : r + 1]
+    spread_line(3, lambda peer: g_mid.at[peer], g_mid_slots)
+    g_mid_slots[along] = g_mid[along]
+
     wait_all(group_recv, 8, e_slots)
     e_mid[...] = sum_slots_of(e_slots)
     spread_line(9, lambda peer: e_mid, e_mid_slots)
@@ -596,7 +640,10 @@
     spread_line(5, lambda peer: g_part, g_parts)
     g_parts[along] = g_part[...]
 
-    first_edges((2, 4))
+    for copy in halos[urgent:]:
+        copy.wait_recv()
+    fill_corners((4,))
+    first_edges((1, 2, 4), (1, 2, 3, 4), (2, 4))
     second((1, 2, 3, 4))
     store = pltpu.make_async_copy(F, out_fields, out_sem)
     store.start()
@@ -744,8 +791,8 @@
             pltpu.SemaphoreType.DMA,
             pltpu.SemaphoreType.DMA,
             pltpu.SemaphoreType.DMA,
-            pltpu.SemaphoreType.DMA((8,)),
-            pltpu.SemaphoreType.DMA((8,)),
+            pltpu.SemaphoreType.DMA((22,)),
+            pltpu.SemaphoreType.DMA((22,)),
             pltpu.SemaphoreType.DMA((11,)),
             pltpu.SemaphoreType.DMA((11,)),
         ],

time: 58.7 us -> 56.8 us (0.968)
  Pallas kernels: 57.2 us -> 55.4 us
    pallas_call x1, Pallas kernels: 42.8 us -> 40.9 us  [front(): pl.pallas_call(functools.partial(front_kernel, sizes), out_shape=(jax.Sha...]
where the time goes in v8:
time: 56.8 us; the launch traced here: 56.7 us
  Pallas kernels  55.4 us (98%)
  between operations  1.29 us (2%)
    pallas_call x1, Pallas kernels, front(): pl.pallas_call(functools.partial(front_kernel, sizes), out_shape=(jax.Sha...  40.9 us
    pallas_call x1, Pallas kernels, tail(): pl.pallas_call(tail_kernel, out_shape=(jax.ShapeDtypeStruct(fields.shape,...  14.4 us

profile of v8, /device:TPU:1, one launch (start us, length us, event | category | flops | bytes accessed | tf_op | source)
XLA Modules:
  0.0 56.7 jit_solution(10391944576740691425)
XLA Ops:
  0.6 0.0 copy-start
  0.6 40.9 %shard_map.94 = (f32[5,16,16,256]{3,2,1,0:T(8,128)}, f32[16,256]{1,0:T(8,128)S(1)}, f32[16,16]{1,0:T(8,128)S(1)}, f32[16,16]{1,0:T(8,128)S(1)}, s32[1,1]{1,0:T(1,128)}, /*index=5*/f32[16,1024]{1,0:T(8,128)S(1)}) custom-call(f32[5,16,16,256]{3,2,1,0:T(8,128)} %fields_hbm.1, f32[1,256]{1,0:T(1,128)} %bitcast.37, f32[1,256]{1,0:T(1,128)} %bitcast.38, ...), custom_call_target="tpu_custom_call" | custom-call | tf_op jit(solution)/shard_map/pallas_call | solution.py:739
  42.2 0.0 copy-done
  42.2 14.4 %shard_map.95 = (f32[5,16,16,256]{3,2,1,0:T(8,128)}, f32[2048,128]{1,0:T(8,128)}, f32[256,256]{1,0:T(8,128)}) custom-call(f32[256,256]{1,0:T(8,128)} %core_ref.1, f32[16,256]{1,0:T(8,128)S(1)} %get-tuple-element.27.coeffs_ref, f32[16,16]{1,0:T(8,128)S(1)} %get-tuple-element.44.factor_ref, f32[16,16]{1,0:T(8,128)S(1)} %get-tuple-element.33.inverse_ref, ...), custom_call_target="tpu_custom_call" | custom-call | tf_op jit(solution)/shard_map/pallas_call | solution.py:211
  (1 shorter events, 0.0 us)
Async XLA Ops:
  0.6 41.6 %copy-start = (f32[4,128,2,256]{3,2,1,0:T(2,128)S(1)}, f32[4,128,2,256]{3,2,1,0:T(2,128)}, u32[]{:S(2)}) copy-start(f32[4,128,2,256]{3,2,1,0:T(2,128)} %param.14) | copy-start | bytes 3145732

commit v9 on v8

--- a/solution.py
+++ b/solution.py
@@ -578,6 +578,13 @@
         for f, new in update(centre, xl, xu, zl, zu, profiles, wanted).items():
             H[f, 1:17, z, :] = new
 
+    wait_all(group_recv, 1, g_slots)
+    total = sum_slots_of(g_slots)
+    for r in range(8):
+        g_mid[r] = total[r : r + 1]
+    spread_line(3, lambda peer: g_mid.at[peer], g_mid_slots)
+    g_mid_slots[along] = g_mid[along]
+
     fill_corners(range(4))
     first_edges((0, 3), (0,), (0, 1, 3))
 
@@ -622,13 +629,6 @@
         late_send[i] = coarse[2 * i : 2 * i + 2]
     spread_z(2, lambda peer: late_send.at[peer], late_slots)
     late_slots[gz] = late_send[gz]
-
-    wait_all(group_recv, 1, g_slots)
-    total = sum_slots_of(g_slots)
-    for r in range(8):
-        g_mid[r] = total[r : r + 1]
-    spread_line(3, lambda peer: g_mid.at[peer], g_mid_slots)
-    g_mid_slots[along] = g_mid[along]
 
     wait_all(group_recv, 8, e_slots)
     e_mid[...] = sum_slots_of(e_slots)

time: 56.8 us -> 54.4 us (0.958)
  Pallas kernels: 55.4 us -> 53 us
    pallas_call x1, Pallas kernels: 40.9 us -> 38.5 us  [front(): pl.pallas_call(functools.partial(front_kernel, sizes), out_shape=(jax.Sha...]
where the time goes in v9:
time: 54.4 us; the launch traced here: 54.3 us
  Pallas kernels  53 us (97%)
  between operations  1.29 us (2%)
    pallas_call x1, Pallas kernels, front(): pl.pallas_call(functools.partial(front_kernel, sizes), out_shape=(jax.Sha...  38.5 us
    pallas_call x1, Pallas kernels, tail(): pl.pallas_call(tail_kernel, out_shape=(jax.ShapeDtypeStruct(fields.shape,...  14.4 us

profile of v9, /device:TPU:1, one launch (start us, length us, event | category | flops | bytes accessed | tf_op | source)
XLA Modules:
  0.0 54.3 jit_solution(2887836201205698250)
XLA Ops:
  0.6 0.0 copy-start
  0.6 38.5 %shard_map.94 = (f32[5,16,16,256]{3,2,1,0:T(8,128)}, f32[16,256]{1,0:T(8,128)S(1)}, f32[16,16]{1,0:T(8,128)S(1)}, f32[16,16]{1,0:T(8,128)S(1)}, s32[1,1]{1,0:T(1,128)}, /*index=5*/f32[16,1024]{1,0:T(8,128)S(1)}) custom-call(f32[5,16,16,256]{3,2,1,0:T(8,128)} %fields_hbm.1, f32[1,256]{1,0:T(1,128)} %bitcast.37, f32[1,256]{1,0:T(1,128)} %bitcast.38, ...), custom_call_target="tpu_custom_call" | custom-call | tf_op jit(solution)/shard_map/pallas_call | solution.py:739
  39.8 0.0 copy-done
  39.8 14.4 %shard_map.95 = (f32[5,16,16,256]{3,2,1,0:T(8,128)}, f32[2048,128]{1,0:T(8,128)}, f32[256,256]{1,0:T(8,128)}) custom-call(f32[256,256]{1,0:T(8,128)} %core_ref.1, f32[16,256]{1,0:T(8,128)S(1)} %get-tuple-element.27.coeffs_ref, f32[16,16]{1,0:T(8,128)S(1)} %get-tuple-element.44.factor_ref, f32[16,16]{1,0:T(8,128)S(1)} %get-tuple-element.33.inverse_ref, ...), custom_call_target="tpu_custom_call" | custom-call | tf_op jit(solution)/shard_map/pallas_call | solution.py:211
  (1 shorter events, 0.0 us)
Async XLA Ops:
  0.6 39.2 %copy-start = (f32[4,128,2,256]{3,2,1,0:T(2,128)S(1)}, f32[4,128,2,256]{3,2,1,0:T(2,128)}, u32[]{:S(2)}) copy-start(f32[4,128,2,256]{3,2,1,0:T(2,128)} %param.14) | copy-start | bytes 3145732

commit v10 on v9

--- a/solution.py
+++ b/solution.py
@@ -630,15 +630,15 @@
     spread_z(2, lambda peer: late_send.at[peer], late_slots)
     late_slots[gz] = late_send[gz]
 
+    wait_all(group_recv, 3, g_mid_slots)
+    g_part[...] = sum_slots_of(g_mid_slots)
+    spread_line(5, lambda peer: g_part, g_parts)
+    g_parts[along] = g_part[...]
+
     wait_all(group_recv, 8, e_slots)
     e_mid[...] = sum_slots_of(e_slots)
     spread_line(9, lambda peer: e_mid, e_mid_slots)
     e_mid_slots[along] = e_mid[...]
-
-    wait_all(group_recv, 3, g_mid_slots)
-    g_part[...] = sum_slots_of(g_mid_slots)
-    spread_line(5, lambda peer: g_part, g_parts)
-    g_parts[along] = g_part[...]
 
     for copy in halos[urgent:]:
         copy.wait_recv()

time: 54.4 us -> 54.4 us (level)
  no operation moved by 1% of the time
where the time goes in v10:
time: 54.4 us; the launch traced here: 54.3 us
  Pallas kernels  53 us (97%)
  between operations  1.29 us (2%)
    pallas_call x1, Pallas kernels, front(): pl.pallas_call(functools.partial(front_kernel, sizes), out_shape=(jax.Sha...  38.5 us
    pallas_call x1, Pallas kernels, tail(): pl.pallas_call(tail_kernel, out_shape=(jax.ShapeDtypeStruct(fields.shape,...  14.4 us

profile of v10, /device:TPU:1, one launch (start us, length us, event | category | flops | bytes accessed | tf_op | source)
XLA Modules:
  0.0 54.3 jit_solution(17026289689228475065)
XLA Ops:
  0.6 0.0 copy-start
  0.6 38.5 %shard_map.94 = (f32[5,16,16,256]{3,2,1,0:T(8,128)}, f32[16,256]{1,0:T(8,128)S(1)}, f32[16,16]{1,0:T(8,128)S(1)}, f32[16,16]{1,0:T(8,128)S(1)}, s32[1,1]{1,0:T(1,128)}, /*index=5*/f32[16,1024]{1,0:T(8,128)S(1)}) custom-call(f32[5,16,16,256]{3,2,1,0:T(8,128)} %fields_hbm.1, f32[1,256]{1,0:T(1,128)} %bitcast.37, f32[1,256]{1,0:T(1,128)} %bitcast.38, ...), custom_call_target="tpu_custom_call" | custom-call | tf_op jit(solution)/shard_map/pallas_call | solution.py:739
  39.8 0.0 copy-done
  39.8 14.4 %shard_map.95 = (f32[5,16,16,256]{3,2,1,0:T(8,128)}, f32[2048,128]{1,0:T(8,128)}, f32[256,256]{1,0:T(8,128)}) custom-call(f32[256,256]{1,0:T(8,128)} %core_ref.1, f32[16,256]{1,0:T(8,128)S(1)} %get-tuple-element.27.coeffs_ref, f32[16,16]{1,0:T(8,128)S(1)} %get-tuple-element.44.factor_ref, f32[16,16]{1,0:T(8,128)S(1)} %get-tuple-element.33.inverse_ref, ...), custom_call_target="tpu_custom_call" | custom-call | tf_op jit(solution)/shard_map/pallas_call | solution.py:211
  (1 shorter events, 0.0 us)
Async XLA Ops:
  0.6 39.2 %copy-start = (f32[4,128,2,256]{3,2,1,0:T(2,128)S(1)}, f32[4,128,2,256]{3,2,1,0:T(2,128)}, u32[]{:S(2)}) copy-start(f32[4,128,2,256]{3,2,1,0:T(2,128)} %param.14) | copy-start | bytes 3145732
